TPU v7x, 32 devices: a whole 2x2x4 slice. The times are simulated.
32 devices in a mesh: groups: 2 (over y), space: 4 (over z), dp: 4 (over x, core).
Axes of the slice: x: 2, y: 2, z: 4, core: 2. Of those that a mesh axis runs over, the one named last changes fastest.
Arguments:
- grad_mid: bfloat16 [8, 8, 180, 768], P(('groups', 'dp'), 'space'), parts along dimension 0, may hold values from -6 to 6
- spectrum: bfloat16 [2, 8, 8, 64, 768], P(None, ('groups', 'dp'), None, 'space'), parts along dimension 1, may hold values from -6 to 6
- filter_inner: bfloat16 [2, 8, 96, 96], replicated, may hold values from -0.4375 to 0.4375
- filter_outer: bfloat16 [2, 8, 96, 96], replicated, may hold values from -0.4375 to 0.4375
- cutoff: int32 [64], replicated, may hold values from 1 to 4, as said below
- normed_mid: bfloat16 [8, 8, 180, 768], P(('groups', 'dp'), 'space'), parts along dimension 0, may hold values from -6 to 6
- hidden_grad: bfloat16 [8, 8, 180, 3072], P(('groups', 'dp'), 'space'), parts along dimension 0, may hold values from -6 to 6
- power_start: bfloat16 [3072, 32], replicated, may hold values from -5 to 5
Outputs:
- grad_input: bfloat16 [8, 8, 180, 768], P(('groups', 'dp'), 'space'), parts along dimension 0
- grad_inner: float32 [4, 8, 96, 96], P('groups', 'dp'), parts along dimension 0
- grad_outer: float32 [4, 8, 96, 96], P('groups', 'dp'), parts along dimension 0
- left_factor: float32 [1536, 32], P('groups'), parts along dimension 0
- right_factor: float32 [6144, 32], P(('groups', 'space', 'dp')), parts along dimension 0
There are 2 independent parts, one for each index of `groups`. A program takes and returns all parts, laid end to end along the dimension named above; an argument that names none is the same for every part. Nothing has to cross between parts.
Inputs may be any that keep to these rules, and one draw needn't show every extreme that they name: A latitude frequency f of longitude mode k is retained where |f| < cutoff[k]; some mode has 4 and some has 1.
All inputs are finite; a program needn't handle non-finite values.
Results may differ from a plain program's by a relative error of at most 0.015.
Values may be sent and summed in bfloat16 or wider, within the bound.
A program may use at most 64 MiB of HBM per device.

v0:
```python
import math

import jax
import jax.numpy as jnp
from jax import lax
from jax.sharding import PartitionSpec as P

D = 768
NB = 8
BS = 96
FF = 3072
LON = 180
KLON = 64


HIGHEST = lax.Precision.HIGHEST


def angle_table(left_count, right_count, length):
    left_index = jnp.arange(left_count, dtype=jnp.int32)[:, None]
    right_index = jnp.arange(right_count, dtype=jnp.int32)[None, :]
    angles = (left_index * right_index % length).astype(jnp.float32) * (2.0 * math.pi / length)
    return (jnp.cos(angles), jnp.sin(angles))


def lon_forward(grid_values, cosine_table, sine_table, factor):
    real_part = jnp.einsum("srlc,kl->srkc", grid_values, cosine_table) * factor
    imag_part = -jnp.einsum("srlc,kl->srkc", grid_values, sine_table) * factor
    return jnp.stack([real_part, imag_part])


def lat_forward(complex_pair, cosine_table, sine_table):
    real_part = jnp.einsum(
        "jt,stkc->sjkc", cosine_table, complex_pair[0]
    ) + jnp.einsum("jt,stkc->sjkc", sine_table, complex_pair[1])
    imag_part = jnp.einsum(
        "jt,stkc->sjkc", cosine_table, complex_pair[1]
    ) - jnp.einsum("jt,stkc->sjkc", sine_table, complex_pair[0])
    return jnp.stack([real_part, imag_part])


def lat_adjoint(complex_pair, cosine_table, sine_table):
    real_part = jnp.einsum(
        "jt,sjkc->stkc", cosine_table, complex_pair[0]
    ) - jnp.einsum("jt,sjkc->stkc", sine_table, complex_pair[1])
    imag_part = jnp.einsum(
        "jt,sjkc->stkc", sine_table, complex_pair[0]
    ) + jnp.einsum("jt,sjkc->stkc", cosine_table, complex_pair[1])
    return jnp.stack([real_part, imag_part])


def lon_adjoint(complex_pair, cosine_table, sine_table, factor):
    summed = jnp.einsum(
        "srkc,kl->srlc", complex_pair[0], cosine_table
    ) - jnp.einsum("srkc,kl->srlc", complex_pair[1], sine_table)
    return summed * factor


def mode_weight(lat_count, first_mode, mode_count, cut_local):
    frequency = jnp.arange(lat_count, dtype=jnp.int32)
    signed = jnp.where(frequency < lat_count // 2, frequency, frequency - lat_count)
    mode_index = first_mode + jnp.arange(mode_count, dtype=jnp.int32)
    double = jnp.where(mode_index == 0, 1.0, 2.0)
    retained = jnp.abs(signed)[:, None] < cut_local[None, :]
    return jnp.where(retained, double[None, :], 0.0).astype(jnp.float32)


def complex_product(real_part, imag_part, weights):
    out_real = jnp.einsum("rbi,bio->rbo", real_part, weights[0]) - jnp.einsum(
        "rbi,bio->rbo", imag_part, weights[1]
    )
    out_imag = jnp.einsum("rbi,bio->rbo", real_part, weights[1]) + jnp.einsum(
        "rbi,bio->rbo", imag_part, weights[0]
    )
    return (out_real, out_imag)


def spectral_filter(real_part, imag_part, inner_weights, outer_weights):
    hidden_real, hidden_imag = complex_product(real_part, imag_part, inner_weights)
    return complex_product(
        jax.nn.gelu(hidden_real, approximate=False),
        jax.nn.gelu(hidden_imag, approximate=False),
        outer_weights,
    )


def filter_backward(spectrum_pair, cotangent, inner_weights, outer_weights):

    def shaped(values):
        return values.reshape(-1, NB, BS)

    outputs, pullback = jax.vjp(
        spectral_filter,
        shaped(spectrum_pair[0]),
        shaped(spectrum_pair[1]),
        inner_weights,
        outer_weights,
    )
    gradients = pullback((shaped(cotangent[0]), shaped(cotangent[1])))
    block_shape = spectrum_pair.shape[1:]
    mode_grad = jnp.stack([gradients[0].reshape(block_shape), gradients[1].reshape(block_shape)])
    return (mode_grad, gradients[2], gradients[3])


def orthonormal(sketch):
    gram_matrix = jnp.dot(sketch.T, sketch, precision=HIGHEST)
    cholesky_factor = jnp.linalg.cholesky(gram_matrix)
    return lax.linalg.triangular_solve(
        cholesky_factor, sketch, left_side=False, lower=True, transpose_a=True
    )


def body(
    grad_mid, spectrum, filter_inner, filter_outer, cutoff, normed_mid, hidden_grad, power_start
):
    space_count = lax.axis_size("space")
    data_count = lax.axis_size("dp")
    sample_count = grad_mid.shape[0]
    lat_count = grad_mid.shape[1] * space_count
    mode_local = KLON // space_count
    factor = 1.0 / math.sqrt(lat_count * LON)
    tokens_mid = normed_mid.reshape(-1, D)
    tokens_grad = hidden_grad.reshape(-1, FF)
    probe = jnp.dot(tokens_grad, power_start, preferred_element_type=jnp.float32).astype(
        jnp.bfloat16
    )
    sketch_local = jnp.dot(tokens_mid.T, probe, preferred_element_type=jnp.float32)
    sketch = lax.psum(sketch_local, ("space", "dp"))
    grad_float = grad_mid.astype(jnp.float32)
    lon_cos, lon_sin = angle_table(KLON, LON, LON)
    lat_cos, lat_sin = angle_table(lat_count, lat_count, lat_count)
    row_spectra = lon_forward(grad_float, lon_cos, lon_sin, factor)
    mode_values = lat_forward(
        lax.all_to_all(
            row_spectra.astype(jnp.bfloat16), "space", split_axis=3, concat_axis=2, tiled=True
        ).astype(jnp.float32),
        lat_cos,
        lat_sin,
    )
    first_mode = lax.axis_index("space") * mode_local
    cut_local = lax.dynamic_slice_in_dim(cutoff, first_mode, mode_local)
    weight = mode_weight(lat_count, first_mode, mode_local, cut_local)
    cotangent = mode_values * weight[None, None, :, :, None]
    mode_grad, inner_grad, outer_grad = filter_backward(
        spectrum.astype(jnp.float32),
        cotangent,
        filter_inner.astype(jnp.float32),
        filter_outer.astype(jnp.float32),
    )
    back = lat_adjoint(mode_grad, lat_cos, lat_sin)
    row_back = lax.all_to_all(
        back.astype(jnp.bfloat16), "space", split_axis=2, concat_axis=3, tiled=True
    ).astype(jnp.float32)
    spectral_grad = lon_adjoint(row_back, lon_cos, lon_sin, factor)
    grad_input = (grad_float + spectral_grad).astype(jnp.bfloat16)
    inner_grad, outer_grad = (
        lax.psum_scatter(
            inner_grad.astype(jnp.bfloat16), "dp", scatter_dimension=1, tiled=True
        ).astype(jnp.float32),
        lax.psum_scatter(
            outer_grad.astype(jnp.bfloat16), "dp", scatter_dimension=1, tiled=True
        ).astype(jnp.float32),
    )
    inner_grad, outer_grad = (
        lax.psum(inner_grad.astype(jnp.bfloat16), "space").astype(jnp.float32),
        lax.psum(outer_grad.astype(jnp.bfloat16), "space").astype(jnp.float32),
    )
    grad_factor = 1.0 / math.sqrt(sample_count * data_count * lat_count * KLON)
    left_factor = orthonormal(sketch)
    left_round = left_factor.astype(jnp.bfloat16)
    mixed = jnp.dot(tokens_mid, left_round, preferred_element_type=jnp.float32).astype(jnp.bfloat16)
    right_sum = lax.psum_scatter(
        jnp.dot(tokens_grad.T, mixed, preferred_element_type=jnp.float32),
        ("space", "dp"),
        scatter_dimension=0,
        tiled=True,
    )
    right_factor = right_sum * (1.0 / math.sqrt(sample_count * data_count * lat_count * LON))
    return (
        grad_input,
        inner_grad * grad_factor,
        outer_grad * grad_factor,
        left_factor,
        right_factor,
    )


def solution(mesh):
    in_specs = (
        P(("groups", "dp"), "space", None, None),
        P(None, ("groups", "dp"), None, "space", None),
        P(),
        P(),
        P(),
        P(("groups", "dp"), "space", None, None),
        P(("groups", "dp"), "space", None, None),
        P(),
    )
    out_specs = (
        P(("groups", "dp"), "space", None, None),
        P("groups", "dp", None, None),
        P("groups", "dp", None, None),
        P("groups", None),
        P(("groups", "space", "dp"), None),
    )
    return jax.shard_map(body, mesh=mesh, in_specs=in_specs, out_specs=out_specs, check_vma=False)
```

profile of v0, /device:TPU:0, one launch (start us, length us, event | category | flops | bytes accessed | tf_op | source)
XLA Modules:
  0.0 245.8 jit_solution(7522442633156601116)
XLA Ops:
  8.0 1.7 fusion.15
  9.7 1.5 fusion.16
  12.5 6.3 %all-to-all-start = ((bf16[2,1,2,64,768]{4,2,1,0,3:T(2,128)(2,1)}), bf16[2,1,2,64,768]{4,2,1,0,3:T(2,128)(2,1)}, u32[]{:S(2)}, u32[]{:S(2)}) async-start(bf16[2,1,2,64,768]{4,2,1,0,3:T(2,128)(2,1)} %copy.97), calls=%async_computation | async-start | bytes 786432 | tf_op jit(solution)/shard_map/all_to_all | solution.py:134
  18.8 2.0 copy.127
  20.8 2.1 reshape.279
  23.1 1.6 convolution_bitcast_fusion.9
  24.8 1.7 fusion.234
  31.2 2.0 reshape_squeeze.13
  36.4 1.5 fusion.32
  40.0 1.5 fusion.30
  46.9 66.7 %all-reduce.16.cloned.1.call-done = f32[768,32]{0,1:T(8,128)} async-done(((f32[768,32]{0,1:T(8,128)}), f32[768,32]{0,1:T(8,128)}) %all-reduce.16.cloned.1.call-update) | async-done | bytes 98320 | tf_op jit(solution)/shard_map/psum | solution.py:128
  113.6 1.8 fusion.239
  115.4 1.4 copy.129
  116.8 1.3 fusion.158
  118.1 4.2 %cholesky.16 = f32[32,32]{1,0:T(8,128)} custom-call(f32[32,32]{1,0:T(8,128)} %fusion.158), custom_call_target="Cholesky" | custom-call | tf_op jit(solution)/shard_map/jit(cholesky)/cholesky | solution.py:107
  123.7 2.0 fusion.155
  125.7 3.8 %custom-call.6 = f32[1,32,32]{1,2,0:T(8,128)} custom-call(f32[1,32,32]{2,1,0:T(8,128)} %fusion.155), custom_call_target="InvertDiagBlocksLowerTriangular" | custom-call | tf_op jit(solution)/shard_map/triangular_solve | solution.py:108
  129.5 1.8 fusion.156
  131.3 2.4 convolution_bitcast_fusion
  133.7 2.6 %copy.149 = f32[3072,32]{1,0:T(8,128)} copy(f32[3072,32]{0,1:T(8,128)} %convolution_bitcast_fusion) | data formatting | bytes 786432
  153.6 3.6 %all-to-all-start.1 = ((bf16[2,1,8,16,768]{4,3,1,0,2:T(8,128)(2,1)}), bf16[2,1,8,16,768]{4,3,1,0,2:T(8,128)(2,1)S(1)}, u32[]{:S(2)}, u32[]{:S(2)}) async-start(bf16[2,1,8,16,768]{4,3,1,0,2:T(8,128)(2,1)} %copy.120), calls=%async_computation.1 | async-start | bytes 786432 | tf_op jit(solution)/shard_map/all_to_all | solution.py:151
  157.2 38.5 %reduce-scatter.6.cloned.1.call-done = f32[192,32]{1,0:T(8,128)} async-done(((f32[3072,32]{1,0:T(8,128)}), f32[192,32]{1,0:T(8,128)}) %reduce-scatter.6.cloned.1.call-update) | async-done | bytes 24592
  196.6 1.6 constant_dynamic-slice_fusion
  198.9 33.5 %all-reduce.20.cloned.1.call-done = (bf16[2,2,96,96]{2,3,1,0:T(8,128)(2,1)}, bf16[2,2,96,96]{2,3,1,0:T(8,128)(2,1)}) async-done(((bf16[2,2,96,96]{2,3,1,0:T(8,128)(2,1)}, bf16[2,2,96,96]{2,3,1,0:T(8,128)(2,1)}), (bf16[2,2,96,96]{2,3,1,0:T(8,128)(2,1)}, bf16[2,2,96,96]{2,3,1,0:T(8,128)(2,1)})) %all-reduce.20.cloned.1.call-update) | async-done | bytes 147472 | tf_op jit(solution)/shard_map/psum | solution.py:165
  (128 shorter events, 41.8 us)
Async XLA Ops:
  8.0 15.1 %copy-start = (bf16[3072,32]{0,1:T(8,128)(2,1)S(1)}, bf16[3072,32]{0,1:T(8,128)(2,1)}, u32[]{:S(2)}) copy-start(bf16[3072,32]{0,1:T(8,128)(2,1)} %param.15) | copy-start | bytes 589828
  8.0 10.8 %copy-start.4 = (bf16[1,2,180,3072]{3,1,2,0:T(2,128)(2,1)S(1)}, bf16[1,2,180,3072]{3,1,2,0:T(2,128)(2,1)}, u32[]{:S(2)}) copy-start(bf16[1,2,180,3072]{3,1,2,0:T(2,128)(2,1)} %param.14) | copy-start | bytes 6635524
  12.5 124.1 %all-to-all-start = ((bf16[2,1,2,64,768]{4,2,1,0,3:T(2,128)(2,1)}), bf16[2,1,2,64,768]{4,2,1,0,3:T(2,128)(2,1)}, u32[]{:S(2)}, u32[]{:S(2)}) async-start(bf16[2,1,2,64,768]{4,2,1,0,3:T(2,128)(2,1)} %copy.97), calls=%async_computation | async-start | bytes 786432 | tf_op jit(solution)/shard_map/all_to_all | solution.py:134
  18.8 94.8 %all-reduce.16.cloned.1.call-start = ((), (), s32[]{:S(2)}) async-start(), calls=%async_computation.3 | async-start | bytes 196608 | tf_op jit(solution)/shard_map/psum | solution.py:128
  20.8 2.1 copy-start.15
  23.1 5.6 %copy-start.1 = (bf16[2,8,96,96]{3,2,1,0:T(8,128)(2,1)S(1)}, bf16[2,8,96,96]{3,2,1,0:T(8,128)(2,1)}, u32[]{:S(2)}) copy-start(bf16[2,8,96,96]{3,2,1,0:T(8,128)(2,1)} %param.10) | copy-start | bytes 884740
  24.8 170.9 %reduce-scatter.6.cloned.1.call-start = ((), (), s32[]{:S(2)}) async-start(), calls=%async_computation.4 | async-start | bytes 1671168
  28.7 2.5 %copy-start.2 = (bf16[128,8,96]{0,2,1:T(8,128)(2,1)}, bf16[128,8,96]{0,2,1:T(8,128)(2,1)S(1)}, u32[]{:S(2)}) copy-start(bf16[128,8,96]{0,2,1:T(8,128)(2,1)S(1)} %copy.92) | copy-start | bytes 589828
  136.4 60.2 %all-reduce.18.cloned.1.call-start = ((), (), s32[]{:S(2)}) async-start(), calls=%async_computation.5 | async-start | bytes 1572864
  137.9 1.7 copy-start.19
  139.7 0.9 copy-start.5
  139.8 1.9 copy-start.6
  140.7 3.1 %copy-start.16 = (bf16[2,8,96,96]{3,2,1,0:T(8,128)(2,1)S(1)}, bf16[2,8,96,96]{3,2,1,0:T(8,128)(2,1)}, u32[]{:S(2)}) copy-start(bf16[2,8,96,96]{3,2,1,0:T(8,128)(2,1)} %param.11) | copy-start | bytes 884740
  141.7 2.3 copy-start.10
  141.7 2.3 copy-start.18
  144.0 1.0 copy-start.3
  145.0 1.4 copy-start.8
  145.0 1.4 copy-start.17
  147.5 1.0 copy-start.12
  147.5 1.1 copy-start.13
  149.7 1.2 copy-start.11
  153.6 82.2 %all-to-all-start.1 = ((bf16[2,1,8,16,768]{4,3,1,0,2:T(8,128)(2,1)}), bf16[2,1,8,16,768]{4,3,1,0,2:T(8,128)(2,1)S(1)}, u32[]{:S(2)}, u32[]{:S(2)}) async-start(bf16[2,1,8,16,768]{4,3,1,0,2:T(8,128)(2,1)} %copy.120), calls=%async_computation.1 | async-start | bytes 786432 | tf_op jit(solution)/shard_map/all_to_all | solution.py:151
  157.2 75.2 %all-reduce.20.cloned.1.call-start = ((), (), s32[]{:S(2)}) async-start(), calls=%async_computation.6 | async-start | bytes 393216 | tf_op jit(solution)/shard_map/psum | solution.py:165
  198.3 38.2 %copy-start.14 = (bf16[1,2,180,768]{3,1,2,0:T(2,128)(2,1)S(1)}, bf16[1,2,180,768]{3,1,2,0:T(2,128)(2,1)}, u32[]{:S(2)}) copy-start(bf16[1,2,180,768]{3,1,2,0:T(2,128)(2,1)} %param.8) | copy-start | bytes 1658884
  (2 other events, 1.5 us)
Sparse Core Ops, SparseCore 0:
  24.9 88.6 all-reduce.15
  136.5 59.0 reduce-scatter.5
Sparse Core Ops, SparseCore 1:
  152.4 37.9 all-reduce.17
  198.4 34.0 all-reduce.19
where the time goes:
time: 247 us; the launch traced here: 246 us
  waiting for transfers between devices  139 us (56%)
  local copies, waits for them, and re-layouts  31.4 us (13%)
  matrix products  26.1 us (11%)
  other arithmetic  22.7 us (9%)
  between operations  16.7 us (7%)
  starting transfers between devices  10.1 us (4%)
    psum x1, waiting for transfers between devices, body(): sketch = lax.psum(sketch_local, ('space', 'dp'))  66.7 us
    unnamed x6, waiting for transfers between devices  38.5 us
    psum x1, waiting for transfers between devices, body(): lax.psum(inner_grad.astype(jnp.bfloat16), 'space').astype(jnp.float32)  33.5 us
    unnamed x49, local copies, waits for them, and re-layouts  13.3 us
    all_to_all x1, starting transfers between devices, body(): lax.all_to_all(row_spectra.astype(jnp.bfloat16), 'space', split_axis=3, c...  6.32 us
    another operation x8, local copies, waits for them, and re-layouts, shaped(): return values.reshape(-1, NB, BS)  6.26 us
    another operation x2, other arithmetic, orthonormal(): lax.linalg.triangular_solve(cholesky_factor, sketch, left_side=False, low...  5.76 us
    another operation x3, other arithmetic, orthonormal(): cholesky_factor = jnp.linalg.cholesky(gram_matrix)  5.62 us
  transfers between devices with their start and end apart: 6, of which 3 were waited for; matrix products, arithmetic and copies ran while one was open for 29% of the time, Pallas kernels for 0%

commit v1 on v0

--- a/solution.py
+++ b/solution.py
@@ -2,7 +2,10 @@
 
 import jax
 import jax.numpy as jnp
+import numpy as np
 from jax import lax
+from jax.experimental import pallas as pl
+from jax.experimental.pallas import tpu as pltpu
 from jax.sharding import PartitionSpec as P
 
 D = 768
@@ -185,6 +188,467 @@
     )
 
 
+def fused_tables(space_count, row_count):
+    lat_count = space_count * row_count
+    mode_local = KLON // space_count
+    factor = 1.0 / math.sqrt(lat_count * LON)
+    angle = (np.outer(np.arange(KLON), np.arange(LON)) % LON) * (2.0 * math.pi / LON)
+    pair = np.stack([np.cos(angle), -np.sin(angle)]) * factor
+    lon_table = (
+        pair.reshape(2, space_count, mode_local, LON)
+        .transpose(1, 0, 2, 3)
+        .reshape(2 * KLON, LON)
+    )
+    spread = np.zeros((row_count, LON, space_count, row_count, 2 * mode_local))
+    for row in range(row_count):
+        spread[row, :, :, row, :] = lon_table.T.reshape(LON, space_count, 2 * mode_local)
+    spread = spread.reshape(row_count, LON, space_count * row_count * 2 * mode_local)
+    angle = (np.outer(np.arange(lat_count), np.arange(lat_count)) % lat_count) * (
+        2.0 * math.pi / lat_count
+    )
+    cosine, sine = np.cos(angle), np.sin(angle)
+    mix = np.stack([np.stack([cosine, sine], -1), np.stack([-sine, cosine], -1)])
+    lat_table = np.einsum("ojti,kl->ojktil", mix, np.eye(mode_local)).reshape(
+        2 * lat_count * mode_local, 2 * lat_count * mode_local
+    )
+    as_bf16 = lambda values: jnp.asarray(values.astype(np.float32), jnp.bfloat16)
+    return as_bf16(lon_table), as_bf16(spread), as_bf16(lat_table), as_bf16(lat_table.T.copy())
+
+
+NN = (((1,), (0,)), ((), ()))
+NT = (((1,), (1,)), ((), ()))
+TN = (((0,), (0,)), ((), ()))
+
+
+def mxu(left, right, dims=NN):
+    return lax.dot_general(left, right, dims, preferred_element_type=jnp.float32)
+
+
+def fused_kernel(
+    grid_hbm,
+    spectrum_hbm,
+    inner_hbm,
+    outer_hbm,
+    cutoff_ref,
+    normed_hbm,
+    hidden_hbm,
+    start_hbm,
+    lon_ref,
+    spread_ref,
+    lat_ref,
+    back_ref,
+    grid_out,
+    weight_out,
+    left_out,
+    right_out,
+    grid_ref,
+    spectrum_ref,
+    inner_ref,
+    outer_ref,
+    normed_ref,
+    hidden_ref,
+    start_ref,
+    inner_wide,
+    outer_wide,
+    act_ref,
+    slope_ref,
+    cot_ref,
+    hid_ref,
+    xg_ref,
+    mode_send,
+    mode_recv,
+    back_send,
+    back_recv,
+    sketch_local,
+    sketch_recv,
+    sketch_part,
+    sketch_cross,
+    sketch_full,
+    right_send,
+    right_recv,
+    right_part,
+    right_cross,
+    wide_send,
+    wide_recv,
+    half_send,
+    half_recv,
+    quarter_send,
+    quarter_recv,
+    piece_all,
+    local_sem,
+    send_sem,
+    recv_sem,
+):
+    bf16, f32 = jnp.bfloat16, jnp.float32
+    space, data = lax.axis_index("space"), lax.axis_index("dp")
+    space_count, data_count = mode_send.shape[0], sketch_recv.shape[0]
+    core, chip = lax.rem(data, 2), lax.div(data, 2)
+    row_count, _, _ = grid_ref.shape
+    slab = mode_send.shape[1] // row_count
+    half = spectrum_ref.shape[0] // 2
+    mode_local = KLON // space_count
+    lat_count = row_count * space_count
+
+    loads = []
+    for index, (source, target) in enumerate(
+        (
+            (grid_hbm, grid_ref),
+            (hidden_hbm, hidden_ref),
+            (start_hbm, start_ref),
+            (normed_hbm, normed_ref),
+            (inner_hbm, inner_ref),
+            (spectrum_hbm, spectrum_ref),
+            (outer_hbm, outer_ref),
+        )
+    ):
+        load = pltpu.make_async_copy(source, target, local_sem.at[index])
+        load.start()
+        loads.append(load)
+
+    barrier = pltpu.get_barrier_semaphore()
+    for step in range(1, space_count):
+        pl.semaphore_signal(
+            barrier,
+            inc=1,
+            device_id={"space": lax.rem(space + step, space_count)},
+            device_id_type=pl.DeviceIdType.MESH,
+        )
+    for step in range(1, data_count):
+        pl.semaphore_signal(
+            barrier,
+            inc=1,
+            device_id={"dp": lax.rem(data + step, data_count)},
+            device_id_type=pl.DeviceIdType.MESH,
+        )
+
+    pending = []
+
+    def push(source, target, device):
+        index = len(pending)
+        copy = pltpu.make_async_remote_copy(
+            src_ref=source,
+            dst_ref=target,
+            send_sem=send_sem.at[index],
+            recv_sem=recv_sem.at[index],
+            device_id=device,
+            device_id_type=pl.DeviceIdType.MESH,
+        )
+        copy.start()
+        pending.append(copy)
+        return copy
+
+    def over_space(source, target):
+        copies = []
+        for step in range(1, space_count):
+            peer = lax.rem(space + step, space_count)
+            copies.append(push(source(peer), target, {"space": peer}))
+        return copies
+
+    def over_data(source, target):
+        copies = []
+        for step in range(1, data_count):
+            peer = lax.rem(data + step, data_count)
+            copies.append(push(source(peer), target, {"dp": peer}))
+        return copies
+
+    def arrive(copies):
+        for copy in copies:
+            copy.wait_recv()
+
+    loads[0].wait()
+    for row in range(row_count):
+        modes = mxu(lon_ref[...], grid_ref[row]).astype(bf16)
+        for peer in range(space_count):
+            mode_send[peer, row * slab : (row + 1) * slab, :] = modes[
+                peer * slab : (peer + 1) * slab
+            ]
+    pl.semaphore_wait(barrier, space_count + data_count - 2)
+    mode_copies = over_space(lambda peer: mode_send.at[peer], mode_recv.at[space])
+    mode_recv[space] = mode_send[space]
+
+    loads[1].wait()
+    loads[2].wait()
+    loads[3].wait()
+    total = None
+    for row in range(row_count):
+        probe = mxu(hidden_ref[row], start_ref[...]).astype(bf16)
+        term = mxu(probe, normed_ref[row], TN)
+        total = term if total is None else total + term
+    rank_part = sketch_local.shape[1]
+    for peer in range(data_count):
+        sketch_local[peer] = total[peer * rank_part : (peer + 1) * rank_part]
+    sketch_copies = over_data(lambda peer: sketch_local.at[peer], sketch_recv.at[data])
+    sketch_recv[data] = sketch_local[data]
+
+    group = 4 * BS
+    column = lax.broadcasted_iota(jnp.int32, (BS, group), 1)
+    place = lax.broadcasted_iota(jnp.int32, (BS, group), 0)
+    repeat = jnp.where(lax.rem(column, BS) == place, 1.0, 0.0).astype(bf16)
+    loads[4].wait()
+    loads[5].wait()
+    loads[6].wait()
+    for source, target in ((inner_ref, inner_wide), (outer_ref, outer_wide)):
+        for block in range(2 * NB):
+            rows = slice(block * BS, (block + 1) * BS)
+            wide = mxu(source[rows, :], repeat)
+            target[rows, :] = jnp.where(lax.div(column, BS) == block % 4, wide, 0.0).astype(bf16)
+
+    def wide_weight(ref, part, index):
+        first = (part * (NB // 4) + index) * group
+        return ref[first : first + group, :]
+
+    groups = [slice(index * group, (index + 1) * group) for index in range(NB // 4)]
+    for index, lanes in enumerate(groups):
+        values = spectrum_ref[:, lanes]
+        by_real = mxu(values, wide_weight(inner_wide, 0, index))
+        by_imag = mxu(values, wide_weight(inner_wide, 1, index))
+        for rows, hidden in (
+            (slice(0, half), by_real[:half] - by_imag[half:]),
+            (slice(half, 2 * half), by_imag[:half] + by_real[half:]),
+        ):
+            cdf = 0.5 * (1.0 + lax.erf(hidden * math.sqrt(0.5)))
+            density = jnp.exp(-0.5 * hidden * hidden) * (1.0 / math.sqrt(2.0 * math.pi))
+            act_ref[rows, lanes] = (hidden * cdf).astype(bf16)
+            slope_ref[rows, lanes] = cdf + hidden * density
+
+    arrive(sketch_copies)
+    part = sketch_recv[0]
+    for peer in range(1, data_count):
+        part = part + sketch_recv[peer]
+    sketch_part[...] = part
+    cross_copies = over_space(lambda peer: sketch_part, sketch_cross.at[space])
+    sketch_cross[space] = part
+
+    full = 2 * half
+    lane = lax.broadcasted_iota(jnp.int32, (full, KLON), 1)
+    row_id = lax.broadcasted_iota(jnp.int32, (full, KLON), 0)
+    mode_id = space * mode_local + lax.rem(row_id, mode_local)
+    own_cut = jnp.where(lane == mode_id, cutoff_ref[...].astype(f32), 0.0)
+    cut = jnp.sum(own_cut, axis=1, keepdims=True)
+    row_id = lax.broadcasted_iota(jnp.int32, (full, 1), 0)
+    frequency = lax.rem(lax.div(row_id, mode_local), lat_count)
+    size = jnp.where(frequency < lat_count // 2, frequency, lat_count - frequency).astype(f32)
+    double = jnp.where(space * mode_local + lax.rem(row_id, mode_local) == 0, 1.0, 2.0)
+    weight = jnp.where(size < cut, double, 0.0)
+
+    arrive(cross_copies)
+    part = sketch_cross[0]
+    for peer in range(1, space_count):
+        part = part + sketch_cross[peer]
+    sketch_full[data] = part
+    full_copies = over_data(lambda peer: sketch_full.at[data], sketch_full.at[data])
+
+    arrive(mode_copies)
+    arrived = mode_recv[...].reshape(full, D)
+    cot_ref[...] = (mxu(lat_ref[...], arrived) * weight).astype(bf16)
+    for index, lanes in enumerate(groups):
+        values = cot_ref[:, lanes]
+        by_real = mxu(values, wide_weight(outer_wide, 0, index), NT)
+        by_imag = mxu(values, wide_weight(outer_wide, 1, index), NT)
+        real = (by_real[:half] + by_imag[half:]) * slope_ref[:half, lanes]
+        imag = (by_real[half:] - by_imag[:half]) * slope_ref[half:, lanes]
+        hid_ref[:half, lanes] = real.astype(bf16)
+        hid_ref[half:, lanes] = imag.astype(bf16)
+        values = hid_ref[:, lanes]
+        by_real = mxu(values, wide_weight(inner_wide, 0, index), NT)
+        by_imag = mxu(values, wide_weight(inner_wide, 1, index), NT)
+        xg_ref[:half, lanes] = (by_real[:half] + by_imag[half:]).astype(bf16)
+        xg_ref[half:, lanes] = (by_real[half:] - by_imag[:half]).astype(bf16)
+    back_send[...] = mxu(back_ref[...], xg_ref[...]).astype(bf16).reshape(back_send.shape)
+    back_copies = over_space(lambda peer: back_send.at[peer], back_recv.at[space])
+    back_recv[space] = back_send[space]
+
+    lane_block = lax.div(lax.broadcasted_iota(jnp.int32, (BS, group), 1), BS)
+    for first, left, right in ((0, spectrum_ref, hid_ref), (2, act_ref, cot_ref)):
+        for index, lanes in enumerate(groups):
+            values = left[:, lanes]
+            turned = jnp.concatenate([right[half:, lanes], -right[:half, lanes]], axis=0)
+            for part, other in ((0, right[:, lanes]), (1, turned)):
+                product = mxu(values, other, TN)
+                compact = jnp.zeros((BS, group), f32)
+                for block in range(4):
+                    compact = jnp.where(
+                        lane_block == block, product[block * BS : (block + 1) * BS], compact
+                    )
+                compact = compact.astype(bf16)
+                rows = slice((first + part) * BS, (first + part + 1) * BS)
+                wide_send[0, index, rows, :] = compact[:, :256]
+                wide_send[1, index, rows, :] = compact[:, 128:]
+    pair = data + 1 - 2 * core
+    core_copy = push(wide_send.at[1 - core], wide_recv, {"dp": pair})
+
+    arrive(full_copies)
+    sketch = sketch_full[...].reshape(data_count * rank_part, D)
+    gram = lax.dot_general(
+        sketch, sketch, NT, precision=HIGHEST, preferred_element_type=f32
+    )
+    rank = sketch.shape[0]
+    rank_row = lax.broadcasted_iota(jnp.int32, (rank, 1), 0)
+    for step in range(rank - 1):
+        pivot = gram[step : step + 1, step : step + 1]
+        ratio = jnp.where(rank_row > step, gram[:, step : step + 1] / pivot, 0.0)
+        sketch = sketch - ratio * sketch[step : step + 1, :]
+        gram = gram - ratio * gram[step : step + 1, :]
+    eye = lax.broadcasted_iota(jnp.int32, (rank, rank), 0) == lax.broadcasted_iota(
+        jnp.int32, (rank, rank), 1
+    )
+    diagonal = jnp.sum(jnp.where(eye, gram, 0.0), axis=1, keepdims=True)
+    left_factor = sketch / jnp.sqrt(diagonal)
+    left_out[...] = left_factor
+    left_round = left_factor.astype(bf16)
+
+    core_copy.wait_recv()
+    mine = wide_send[core].astype(f32) + wide_recv[...].astype(f32)
+    wide_recv[...] = mine.astype(bf16)
+    chip_copy = push(wide_recv.at[1 - chip], half_recv, {"dp": lax.rem(data + 2, data_count)})
+
+    total = None
+    for row in range(row_count):
+        mixed = mxu(left_round, normed_ref[row], NT).astype(bf16)
+        term = mxu(mixed, hidden_ref[row])
+        total = term if total is None else total + term
+    total = total.astype(bf16)
+    share = FF // (space_count * data_count)
+    for owner in range(space_count * data_count):
+        first = owner * share // 128 * 128
+        right_send[owner % data_count, owner // data_count] = total[:, first : first + 256]
+    right_copies = over_data(lambda peer: right_send.at[peer], right_recv.at[data])
+    right_recv[data] = right_send[data]
+
+    chip_copy.wait_recv()
+    mine = wide_recv[chip].astype(f32) + half_recv[...].astype(f32)
+    quarter_send[...] = mine.astype(bf16).reshape(quarter_send.shape)
+    quarter_copies = over_space(lambda peer: quarter_send.at[peer], quarter_recv.at[space])
+    quarter_recv[space] = quarter_send[space]
+
+    arrive(right_copies)
+    part = right_recv[0].astype(f32)
+    for peer in range(1, data_count):
+        part = part + right_recv[peer].astype(f32)
+    right_part[...] = part.astype(bf16)
+    last_copies = over_space(lambda peer: right_part.at[peer], right_cross.at[space])
+    right_cross[space] = right_part[space]
+
+    arrive(back_copies)
+    arrived = back_recv[...].reshape(full, D)
+    for row in range(row_count):
+        grid_out[row] = (
+            grid_ref[row].astype(f32) + mxu(spread_ref[row], arrived)
+        ).astype(bf16)
+
+    arrive(quarter_copies)
+    part = quarter_recv[0].astype(f32)
+    for peer in range(1, space_count):
+        part = part + quarter_recv[peer].astype(f32)
+    piece_all[space] = part.astype(bf16)
+    piece_copies = over_space(lambda peer: piece_all.at[space], piece_all.at[space])
+
+    arrive(last_copies)
+    part = right_cross[0].astype(f32)
+    for peer in range(1, space_count):
+        part = part + right_cross[peer].astype(f32)
+    tokens = data_count * lat_count * LON
+    right_out[...] = part * (1.0 / math.sqrt(tokens))
+
+    arrive(piece_copies)
+    modes = data_count * lat_count * KLON
+    weight_out[...] = piece_all[...].astype(f32).reshape(weight_out.shape) * (
+        1.0 / math.sqrt(modes)
+    )
+    for copy in pending:
+        copy.wait_send()
+
+
+def fused_body(
+    grad_mid, spectrum, filter_inner, filter_outer, cutoff, normed_mid, hidden_grad, power_start
+):
+    space_count = lax.axis_size("space")
+    data_count = lax.axis_size("dp")
+    row_count = grad_mid.shape[1]
+    mode_local = KLON // space_count
+    modes = 2 * row_count * space_count * mode_local
+    rank = power_start.shape[1]
+    bf16, f32 = jnp.bfloat16, jnp.float32
+    lon_table, spread, lat_table, back_table = fused_tables(space_count, row_count)
+    vmem = pl.BlockSpec(memory_space=pltpu.VMEM)
+    anywhere = pl.BlockSpec(memory_space=pl.ANY)
+    slab = (space_count, row_count * 2 * mode_local, D)
+    copies = 5 * (space_count - 1) + 3 * (data_count - 1) + 2 + (space_count - 1)
+    grid_out, weight_out, left_out, right_out = pl.pallas_call(
+        fused_kernel,
+        out_shape=(
+            jax.ShapeDtypeStruct((row_count, LON, D), bf16),
+            jax.ShapeDtypeStruct((4 * BS, 256), f32),
+            jax.ShapeDtypeStruct((rank, D), f32),
+            jax.ShapeDtypeStruct((rank, 256), f32),
+        ),
+        in_specs=[anywhere] * 4 + [vmem] + [anywhere] * 3 + [vmem] * 4,
+        out_specs=(vmem,) * 4,
+        scratch_shapes=[
+            pltpu.VMEM((row_count, LON, D), bf16),
+            pltpu.VMEM((modes, D), bf16),
+            pltpu.VMEM((2 * NB * BS, BS), bf16),
+            pltpu.VMEM((2 * NB * BS, BS), bf16),
+            pltpu.VMEM((row_count, LON, D), bf16),
+            pltpu.VMEM((row_count, LON, FF), bf16),
+            pltpu.VMEM((FF, rank), bf16),
+            pltpu.VMEM((2 * NB * BS, 4 * BS), bf16),
+            pltpu.VMEM((2 * NB * BS, 4 * BS), bf16),
+            pltpu.VMEM((modes, D), bf16),
+            pltpu.VMEM((modes, D), f32),
+            pltpu.VMEM((modes, D), bf16),
+            pltpu.VMEM((modes, D), bf16),
+            pltpu.VMEM((modes, D), bf16),
+            pltpu.VMEM(slab, bf16),
+            pltpu.VMEM(slab, bf16),
+            pltpu.VMEM(slab, bf16),
+            pltpu.VMEM(slab, bf16),
+            pltpu.VMEM((data_count, rank // data_count, D), f32),
+            pltpu.VMEM((data_count, rank // data_count, D), f32),
+            pltpu.VMEM((rank // data_count, D), f32),
+            pltpu.VMEM((space_count, rank // data_count, D), f32),
+            pltpu.VMEM((data_count, rank // data_count, D), f32),
+            pltpu.VMEM((data_count, space_count, rank, 256), bf16),
+            pltpu.VMEM((data_count, space_count, rank, 256), bf16),
+            pltpu.VMEM((space_count, rank, 256), bf16),
+            pltpu.VMEM((space_count, rank, 256), bf16),
+            pltpu.VMEM((2, 2, 4 * BS, 256), bf16),
+            pltpu.VMEM((2, 4 * BS, 256), bf16),
+            pltpu.VMEM((4 * BS, 256), bf16),
+            pltpu.VMEM((4 * BS, 256), bf16),
+            pltpu.VMEM((space_count, 4 * BS // space_count, 256), bf16),
+            pltpu.VMEM((space_count, 4 * BS // space_count, 256), bf16),
+            pltpu.VMEM((space_count, 4 * BS // space_count, 256), bf16),
+            pltpu.SemaphoreType.DMA((7,)),
+            pltpu.SemaphoreType.DMA((copies,)),
+            pltpu.SemaphoreType.DMA((copies,)),
+        ],
+        compiler_params=pltpu.CompilerParams(
+            collective_id=0, has_side_effects=True, vmem_limit_bytes=48 * 1024 * 1024
+        ),
+        name="fused_filter_sketch",
+    )(
+        grad_mid.reshape(row_count, LON, D),
+        spectrum.reshape(modes, D),
+        filter_inner.reshape(2 * NB * BS, BS),
+        filter_outer.reshape(2 * NB * BS, BS),
+        cutoff.reshape(1, KLON),
+        normed_mid.reshape(row_count, LON, D),
+        hidden_grad.reshape(row_count, LON, FF),
+        power_start,
+        lon_table,
+        spread,
+        lat_table,
+        back_table,
+    )
+    odd = lax.rem(lax.axis_index("dp"), 2) == 1
+    width = 2 * BS
+    weights = jnp.where(odd, weight_out[:, 256 - width :], weight_out[:, :width])
+    weights = weights.reshape(4, BS, 2, BS).transpose(0, 2, 1, 3)
+    right = jnp.where(odd, right_out[:, 256 - width :], right_out[:, :width])
+    return (grid_out.reshape(grad_mid.shape), weights[:2], weights[2:], left_out.T, right.T)
+
+
 def solution(mesh):
     in_specs = (
         P(("groups", "dp"), "space", None, None),
@@ -203,4 +667,6 @@
         P("groups", None),
         P(("groups", "space", "dp"), None),
     )
-    return jax.shard_map(body, mesh=mesh, in_specs=in_specs, out_specs=out_specs, check_vma=False)
+    fits = mesh.shape["space"] == 4 and mesh.shape["dp"] == 4
+    chosen = fused_body if fits else body
+    return jax.shard_map(chosen, mesh=mesh, in_specs=in_specs, out_specs=out_specs, check_vma=False)

time: 247 us -> 55.3 us (0.22)
  waiting for transfers between devices: 139 us -> 0 us
  Pallas kernels: 0 us -> 41.6 us
  matrix products: 26.1 us -> 0 us
  other arithmetic: 22.7 us -> 0.86 us
  local copies, waits for them, and re-layouts: 31.4 us -> 11.9 us
  between operations: 16.7 us -> 0.76 us
  starting transfers between devices: 10.1 us -> 0 us
    psum x2 -> x0, waiting for transfers between devices: 100 us -> none  [the longest x1 66.7 us: body(): sketch = lax.psum(sketch_local, ('space', 'dp'))]
    pallas_call x0 -> x1, Pallas kernels: none -> 41.6 us  [fused_body(): pl.pallas_call(fused_kernel, out_shape=(jax.ShapeDtypeStruct((row_count,...]
    unnamed x6 -> x0, waiting for transfers between devices: 38.5 us -> none
    dot_general x35 -> x0, matrix products: 24.3 us -> none  [the longest x5 4.52 us: complex_product(): jnp.einsum('rbi,bio->rbo', imag_part, weights[1])]
    another operation x9 -> x0, other arithmetic: 12.9 us -> none  [the longest x2 5.76 us: orthonormal(): lax.linalg.triangular_solve(cholesky_factor, sketch, left_side=False, low...]
    all_to_all x2 -> x0, starting transfers between devices: 9.88 us -> none  [the longest x1 6.32 us: body(): lax.all_to_all(row_spectra.astype(jnp.bfloat16), 'space', split_axis=3, c...]
    another operation x14 -> x0, local copies, waits for them, and re-layouts: 8.82 us -> none  [the longest x8 6.26 us: shaped(): return values.reshape(-1, NB, BS)]
    mul x6 -> x0, other arithmetic: 5.59 us -> none  [the longest x1 1.52 us: spectral_filter(): jax.nn.gelu(hidden_real, approximate=False)]
  transfers between devices with their start and end apart: 6 -> 0, of which waited for: 3 -> 0; matrix products, arithmetic and copies ran while one was open for 29% -> 0% of each run, Pallas kernels for 0% -> 0%
where the time goes in v1:
time: 55.3 us; the launch traced here: 55.1 us
  Pallas kernels  41.6 us (75%)
  local copies, waits for them, and re-layouts  11.9 us (22%)
  other arithmetic  0.86 us (2%)
  between operations  0.76 us (1%)
    pallas_call x1, Pallas kernels, fused_body(): pl.pallas_call(fused_kernel, out_shape=(jax.ShapeDtypeStruct((row_count,...  41.6 us
    unnamed x30, local copies, waits for them, and re-layouts  9.83 us
    reshape x1, local copies, waits for them, and re-layouts, fused_body(): normed_mid.reshape(row_count, LON, D)  1.48 us

profile of v1, /device:TPU:0, one launch (start us, length us, event | category | flops | bytes accessed | tf_op | source)
XLA Modules:
  0.0 55.1 jit_solution(17992596746028530344)
XLA Ops:
  0.6 0.0 copy-start.10
  0.6 1.5 %copy_bitcast_fusion.1 = (bf16[2,180,768]{2,1,0:T(8,128)(2,1)S(1)}, bf16[2,180,768]{2,1,0:T(8,128)(2,1)S(1)}) fusion(bf16[1,2,180,768]{3,1,2,0:T(2,128)(2,1)} %param.17, bf16[1,2,180,768]{3,1,2,0:T(2,128)(2,1)} %param.12), kind=kLoop, calls=%fused_computation.1 | loop fusion | bytes 2211840 | tf_op jit(solution)/shard_map/reshape | solution.py:636
  2.1 0.0 copy-start.11
  2.1 0.4 copy-done.10
  2.6 1.9 %copy.34 = bf16[1,2,180,3072]{3,2,1,0:T(8,128)(2,1)} copy(bf16[1,2,180,3072]{3,1,2,0:T(2,128)(2,1)S(1)} %copy-done.10) | data formatting | bytes 4423680 | tf_op args[6]
  4.5 0.0 copy-done.11
  4.5 0.4 copy.26.start_hbm
  4.9 0.0 copy-done
  5.0 0.0 copy-start.3
  5.0 0.9 %copy-done.3 = bf16[2,180,256]{2,1,0:T(8,128)(2,1)S(1)} copy-done((bf16[2,180,256]{2,1,0:T(8,128)(2,1)S(1)}, bf16[2,180,256]{2,1,0:T(8,128)(2,1)}, u32[]{:S(2)}) %copy-start.3) | copy-done | bytes 184344
  5.9 0.9 %copy-done.4 = bf16[256,256]{1,0:T(8,128)(2,1)S(1)} copy-done((bf16[256,256]{1,0:T(8,128)(2,1)S(1)}, bf16[256,256]{1,0:T(8,128)(2,1)}, u32[]{:S(2)}) %copy-start.4) | copy-done | bytes 131096
  6.8 0.9 %copy-done.5 = bf16[256,256]{1,0:T(8,128)(2,1)S(1)} copy-done((bf16[256,256]{1,0:T(8,128)(2,1)S(1)}, bf16[256,256]{1,0:T(8,128)(2,1)}, u32[]{:S(2)}) %copy-start.5) | copy-done | bytes 131096
  7.7 0.8 %copy-done.8 = bf16[128,180]{1,0:T(8,128)(2,1)S(1)} copy-done((bf16[128,180]{1,0:T(8,128)(2,1)S(1)}, bf16[128,180]{1,0:T(8,128)(2,1)}, u32[]{:S(2)}) %copy-start.8) | copy-done | bytes 46104
  8.5 41.6 %fused_filter_sketch.1 = (bf16[2,180,768]{2,1,0:T(8,128)(2,1)S(1)}, f32[384,256]{1,0:T(8,128)S(1)}, f32[32,768]{1,0:T(8,128)S(1)}, f32[32,256]{1,0:T(8,128)S(1)}) custom-call(bf16[2,180,768]{2,1,0:T(8,128)(2,1)S(1)} %get-tuple-element.26.grid_hbm, bf16[256,768]{1,0:T(8,128)(2,1)S(1)} %bitcast.19, bf16[1536,96]{1,0:T(8,128)(2,1)S(1)} %bitcast.20, ...), custom_call_target="tpu_custom_call" | custom-call | tf_op jit(solution)/shard_map/fused_filter_sketch/pallas_call | solution.py:577
  50.1 0.0 copy-start.6
  50.1 1.2 %copy.28 = bf16[1,2,180,768]{3,1,2,0:T(2,128)(2,1)} copy(bf16[1,2,180,768]{3,2,1,0:T(8,128)(2,1)S(1)} %bitcast.18) | data formatting | bytes 1105920
  51.4 0.2 slice_select_fusion
  51.5 0.1 copy.27
  51.7 0.3 reshape.45
  52.0 0.2 fusion
  52.1 0.8 %copy.29 = f32[2,2,96,96]{3,2,1,0:T(8,128)} copy(f32[2,2,96,96]{2,0,3,1:T(2,128)S(1)} %get-tuple-element.24) | data formatting | bytes 294912
  52.9 0.8 %copy.30 = f32[2,2,96,96]{3,2,1,0:T(8,128)} copy(f32[2,2,96,96]{2,0,3,1:T(2,128)S(1)} %get-tuple-element.23) | data formatting | bytes 294912
  53.7 0.7 %select_bitcast_fusion = f32[192,32]{0,1:T(8,128)} fusion(f32[32,256]{1,0:T(8,128)S(1)} %get-tuple-element.12, pred[]{:T(512)S(6)} %eq.3), kind=kLoop, calls=%fused_computation.4 | loop fusion | flops 6144 | bytes 73729 | tf_op jit(solution)/shard_map/transpose | solution.py:649
  54.4 0.6 %copy.36 = f32[768,32]{0,1:T(8,128)} copy(f32[768,32]{0,1:T(8,128)S(1)} %bitcast.22) | data formatting | bytes 196608
  (13 shorter events, 0.0 us)
Async XLA Ops:
  0.6 2.0 %copy-start.10 = (bf16[1,2,180,3072]{3,1,2,0:T(2,128)(2,1)S(1)}, bf16[1,2,180,3072]{3,1,2,0:T(2,128)(2,1)}, u32[]{:S(2)}) copy-start(bf16[1,2,180,3072]{3,1,2,0:T(2,128)(2,1)} %param.18) | copy-start | bytes 6635524
  2.1 2.4 %copy-start.11 = (bf16[3072,32]{0,1:T(8,128)(2,1)S(1)}, bf16[3072,32]{0,1:T(8,128)(2,1)}, u32[]{:S(2)}) copy-start(bf16[3072,32]{0,1:T(8,128)(2,1)} %param.19) | copy-start | bytes 589828
  2.6 2.3 %copy-start = (bf16[2,1,8,16,768]{4,3,2,1,0:T(8,128)(2,1)S(1)}, bf16[2,1,8,16,768]{4,3,2,1,0:T(8,128)(2,1)}, u32[]{:S(2)}) copy-start(bf16[2,1,8,16,768]{4,3,2,1,0:T(8,128)(2,1)} %param.13) | copy-start | bytes 1179652
  2.6 2.3 %copy-start.1 = (bf16[2,8,96,96]{3,2,1,0:T(8,128)(2,1)S(1)}, bf16[2,8,96,96]{3,2,1,0:T(8,128)(2,1)}, u32[]{:S(2)}) copy-start(bf16[2,8,96,96]{3,2,1,0:T(8,128)(2,1)} %param.14) | copy-start | bytes 884740
  2.6 2.3 %copy-start.2 = (bf16[2,8,96,96]{3,2,1,0:T(8,128)(2,1)S(1)}, bf16[2,8,96,96]{3,2,1,0:T(8,128)(2,1)}, u32[]{:S(2)}) copy-start(bf16[2,8,96,96]{3,2,1,0:T(8,128)(2,1)} %param.15) | copy-start | bytes 884740
  2.6 2.4 %copy-start.9 = (s32[64]{0:T(128)S(1)}, s32[64]{0:T(128)}, u32[]{:S(2)}) copy-start(s32[64]{0:T(128)} %param.16) | copy-start | bytes 772
  5.0 0.9 %copy-start.3 = (bf16[2,180,256]{2,1,0:T(8,128)(2,1)S(1)}, bf16[2,180,256]{2,1,0:T(8,128)(2,1)}, u32[]{:S(2)}) copy-start(bf16[2,180,256]{2,1,0:T(8,128)(2,1)} %constant.19.clone.spread_ref) | copy-start | bytes 552964
  5.9 0.9 %copy-start.4 = (bf16[256,256]{1,0:T(8,128)(2,1)S(1)}, bf16[256,256]{1,0:T(8,128)(2,1)}, u32[]{:S(2)}) copy-start(bf16[256,256]{1,0:T(8,128)(2,1)} %constant.20.clone.lat_ref) | copy-start | bytes 393220
  6.8 0.9 %copy-start.5 = (bf16[256,256]{1,0:T(8,128)(2,1)S(1)}, bf16[256,256]{1,0:T(8,128)(2,1)}, u32[]{:S(2)}) copy-start(bf16[256,256]{1,0:T(8,128)(2,1)} %constant.21.clone.back_ref) | copy-start | bytes 393220
  7.7 0.8 %copy-start.8 = (bf16[128,180]{1,0:T(8,128)(2,1)S(1)}, bf16[128,180]{1,0:T(8,128)(2,1)}, u32[]{:S(2)}) copy-start(bf16[128,180]{1,0:T(8,128)(2,1)} %constant.18.clone.lon_ref) | copy-start | bytes 138244
  50.1 1.2 %copy-start.6 = (f32[32,768]{1,0:T(8,128)}, f32[32,768]{1,0:T(8,128)S(1)}, u32[]{:S(2)}) copy-start(f32[32,768]{1,0:T(8,128)S(1)} %get-tuple-element.11) | copy-start | bytes 294916
  51.4 3.1 %copy-start.7 = (f32[32,768]{1,0:T(8,128)S(1)}, f32[32,768]{1,0:T(8,128)}, u32[]{:S(2)}) copy-start(f32[32,768]{1,0:T(8,128)} %copy-done.6) | copy-start | bytes 294916

commit v2 on v1

--- a/solution.py
+++ b/solution.py
@@ -199,10 +199,10 @@
         .transpose(1, 0, 2, 3)
         .reshape(2 * KLON, LON)
     )
-    spread = np.zeros((row_count, LON, space_count, row_count, 2 * mode_local))
+    spread = np.zeros((LON, row_count, space_count, row_count, 2 * mode_local))
     for row in range(row_count):
-        spread[row, :, :, row, :] = lon_table.T.reshape(LON, space_count, 2 * mode_local)
-    spread = spread.reshape(row_count, LON, space_count * row_count * 2 * mode_local)
+        spread[:, row, :, row, :] = lon_table.T.reshape(LON, space_count, 2 * mode_local)
+    spread = spread.reshape(LON * row_count, space_count * row_count * 2 * mode_local)
     angle = (np.outer(np.arange(lat_count), np.arange(lat_count)) % lat_count) * (
         2.0 * math.pi / lat_count
     )
@@ -212,7 +212,7 @@
         2 * lat_count * mode_local, 2 * lat_count * mode_local
     )
     as_bf16 = lambda values: jnp.asarray(values.astype(np.float32), jnp.bfloat16)
-    return as_bf16(lon_table), as_bf16(spread), as_bf16(lat_table), as_bf16(lat_table.T.copy())
+    return as_bf16(spread.T.copy()), as_bf16(spread), as_bf16(lat_table), as_bf16(lat_table.T.copy())
 
 
 NN = (((1,), (0,)), ((), ()))
@@ -233,14 +233,20 @@
     normed_hbm,
     hidden_hbm,
     start_hbm,
+    lon_hbm,
+    spread_hbm,
+    lat_hbm,
+    back_hbm,
+    grid_hbm_out,
+    weight_out,
+    left_out,
+    scale_out,
+    right_out,
     lon_ref,
     spread_ref,
     lat_ref,
     back_ref,
     grid_out,
-    weight_out,
-    left_out,
-    right_out,
     grid_ref,
     spectrum_ref,
     inner_ref,
@@ -283,27 +289,49 @@
     space, data = lax.axis_index("space"), lax.axis_index("dp")
     space_count, data_count = mode_send.shape[0], sketch_recv.shape[0]
     core, chip = lax.rem(data, 2), lax.div(data, 2)
-    row_count, _, _ = grid_ref.shape
-    slab = mode_send.shape[1] // row_count
+    row_count = grid_ref.shape[2]
+    token_count = grid_ref.shape[1] * row_count
     half = spectrum_ref.shape[0] // 2
     mode_local = KLON // space_count
     lat_count = row_count * space_count
 
-    loads = []
-    for index, (source, target) in enumerate(
-        (
-            (grid_hbm, grid_ref),
-            (hidden_hbm, hidden_ref),
-            (start_hbm, start_ref),
-            (normed_hbm, normed_ref),
+    used = 0
+
+    def load(source, target):
+        nonlocal used
+        copy = pltpu.make_async_copy(source, target, local_sem.at[used])
+        copy.start()
+        used += 1
+        return copy
+
+    def load_tokens(source, target):
+        return [
+            load(source.at[:, :, index * 128 : (index + 1) * 128], target.at[index])
+            for index in range(target.shape[0])
+        ]
+
+    def finish(copies):
+        for copy in copies:
+            copy.wait()
+
+    def tokens(ref):
+        view = ref.reshape(ref.shape[0], token_count, 128)
+        return jnp.concatenate([view[index] for index in range(ref.shape[0])], axis=1)
+
+    grid_loads = load_tokens(grid_hbm, grid_ref) + [load(lon_hbm, lon_ref)]
+    hidden_loads = load_tokens(hidden_hbm, hidden_ref) + [load(start_hbm, start_ref)]
+    normed_loads = load_tokens(normed_hbm, normed_ref)
+    other_loads = [
+        load(source, target)
+        for source, target in (
             (inner_hbm, inner_ref),
             (spectrum_hbm, spectrum_ref),
             (outer_hbm, outer_ref),
+            (lat_hbm, lat_ref),
+            (back_hbm, back_ref),
+            (spread_hbm, spread_ref),
         )
-    ):
-        load = pltpu.make_async_copy(source, target, local_sem.at[index])
-        load.start()
-        loads.append(load)
+    ]
 
     barrier = pltpu.get_barrier_semaphore()
     for step in range(1, space_count):
@@ -355,25 +383,16 @@
         for copy in copies:
             copy.wait_recv()
 
-    loads[0].wait()
-    for row in range(row_count):
-        modes = mxu(lon_ref[...], grid_ref[row]).astype(bf16)
-        for peer in range(space_count):
-            mode_send[peer, row * slab : (row + 1) * slab, :] = modes[
-                peer * slab : (peer + 1) * slab
-            ]
+    finish(grid_loads)
+    mode_send[...] = mxu(lon_ref[...], tokens(grid_ref)).astype(bf16).reshape(mode_send.shape)
     pl.semaphore_wait(barrier, space_count + data_count - 2)
     mode_copies = over_space(lambda peer: mode_send.at[peer], mode_recv.at[space])
     mode_recv[space] = mode_send[space]
 
-    loads[1].wait()
-    loads[2].wait()
-    loads[3].wait()
-    total = None
-    for row in range(row_count):
-        probe = mxu(hidden_ref[row], start_ref[...]).astype(bf16)
-        term = mxu(probe, normed_ref[row], TN)
-        total = term if total is None else total + term
+    finish(hidden_loads)
+    probe = mxu(tokens(hidden_ref), start_ref[...], NT).astype(bf16)
+    finish(normed_loads)
+    total = mxu(probe, tokens(normed_ref), TN)
     rank_part = sketch_local.shape[1]
     for peer in range(data_count):
         sketch_local[peer] = total[peer * rank_part : (peer + 1) * rank_part]
@@ -384,9 +403,7 @@
     column = lax.broadcasted_iota(jnp.int32, (BS, group), 1)
     place = lax.broadcasted_iota(jnp.int32, (BS, group), 0)
     repeat = jnp.where(lax.rem(column, BS) == place, 1.0, 0.0).astype(bf16)
-    loads[4].wait()
-    loads[5].wait()
-    loads[6].wait()
+    finish(other_loads)
     for source, target in ((inner_ref, inner_wide), (outer_ref, outer_wide)):
         for block in range(2 * NB):
             rows = slice(block * BS, (block + 1) * BS)
@@ -493,21 +510,18 @@
         jnp.int32, (rank, rank), 1
     )
     diagonal = jnp.sum(jnp.where(eye, gram, 0.0), axis=1, keepdims=True)
-    left_factor = sketch / jnp.sqrt(diagonal)
-    left_out[...] = left_factor
-    left_round = left_factor.astype(bf16)
+    scale = 1.0 / jnp.sqrt(diagonal)
+    left_out[...] = sketch
+    scale_out[...] = scale
+    left_round = (sketch * scale).astype(bf16)
 
     core_copy.wait_recv()
     mine = wide_send[core].astype(f32) + wide_recv[...].astype(f32)
     wide_recv[...] = mine.astype(bf16)
     chip_copy = push(wide_recv.at[1 - chip], half_recv, {"dp": lax.rem(data + 2, data_count)})
 
-    total = None
-    for row in range(row_count):
-        mixed = mxu(left_round, normed_ref[row], NT).astype(bf16)
-        term = mxu(mixed, hidden_ref[row])
-        total = term if total is None else total + term
-    total = total.astype(bf16)
+    mixed = mxu(left_round, tokens(normed_ref), NT).astype(bf16)
+    total = mxu(mixed, tokens(hidden_ref)).astype(bf16)
     share = FF // (space_count * data_count)
     for owner in range(space_count * data_count):
         first = owner * share // 128 * 128
@@ -531,10 +545,14 @@
 
     arrive(back_copies)
     arrived = back_recv[...].reshape(full, D)
-    for row in range(row_count):
-        grid_out[row] = (
-            grid_ref[row].astype(f32) + mxu(spread_ref[row], arrived)
-        ).astype(bf16)
+    grid_view = grid_out.reshape(grid_out.shape[0], token_count, 128)
+    result = (tokens(grid_ref).astype(f32) + mxu(spread_ref[...], arrived)).astype(bf16)
+    for index in range(grid_out.shape[0]):
+        grid_view[index] = result[:, index * 128 : (index + 1) * 128]
+    stores = [
+        load(grid_out.at[index], grid_hbm_out.at[:, :, index * 128 : (index + 1) * 128])
+        for index in range(grid_out.shape[0])
+    ]
 
     arrive(quarter_copies)
     part = quarter_recv[0].astype(f32)
@@ -547,14 +565,16 @@
     part = right_cross[0].astype(f32)
     for peer in range(1, space_count):
         part = part + right_cross[peer].astype(f32)
-    tokens = data_count * lat_count * LON
-    right_out[...] = part * (1.0 / math.sqrt(tokens))
+    part = jnp.where(core == 1, pltpu.roll(part, 192, 1), part)
+    right_out[...] = part[:, : 2 * BS]
 
     arrive(piece_copies)
-    modes = data_count * lat_count * KLON
-    weight_out[...] = piece_all[...].astype(f32).reshape(weight_out.shape) * (
-        1.0 / math.sqrt(modes)
-    )
+    for index in range(space_count):
+        part = piece_all[index].astype(f32)
+        part = jnp.where(core == 1, pltpu.roll(part, 192, 1), part)
+        weight_out[index, 0] = part[:, :BS]
+        weight_out[index, 1] = pltpu.roll(part, 256 - BS, 1)[:, :BS]
+    finish(stores)
     for copy in pending:
         copy.wait_send()
 
@@ -574,24 +594,31 @@
     anywhere = pl.BlockSpec(memory_space=pl.ANY)
     slab = (space_count, row_count * 2 * mode_local, D)
     copies = 5 * (space_count - 1) + 3 * (data_count - 1) + 2 + (space_count - 1)
-    grid_out, weight_out, left_out, right_out = pl.pallas_call(
+    grid_shape = (D // 128, LON, row_count, 128)
+    grid_out, weight_out, left_out, scale_out, right_out = pl.pallas_call(
         fused_kernel,
         out_shape=(
-            jax.ShapeDtypeStruct((row_count, LON, D), bf16),
-            jax.ShapeDtypeStruct((4 * BS, 256), f32),
+            jax.ShapeDtypeStruct((LON, row_count, D), bf16),
+            jax.ShapeDtypeStruct((4, 2, BS, BS), f32),
             jax.ShapeDtypeStruct((rank, D), f32),
-            jax.ShapeDtypeStruct((rank, 256), f32),
+            jax.ShapeDtypeStruct((rank, 1), f32),
+            jax.ShapeDtypeStruct((rank, 2 * BS), f32),
         ),
-        in_specs=[anywhere] * 4 + [vmem] + [anywhere] * 3 + [vmem] * 4,
-        out_specs=(vmem,) * 4,
+        in_specs=[anywhere] * 4 + [vmem] + [anywhere] * 7,
+        out_specs=(anywhere,) + (vmem,) * 4,
         scratch_shapes=[
-            pltpu.VMEM((row_count, LON, D), bf16),
+            pltpu.VMEM((modes, LON * row_count), bf16),
+            pltpu.VMEM((LON * row_count, modes), bf16),
+            pltpu.VMEM((modes, modes), bf16),
+            pltpu.VMEM((modes, modes), bf16),
+            pltpu.VMEM(grid_shape, bf16),
+            pltpu.VMEM(grid_shape, bf16),
             pltpu.VMEM((modes, D), bf16),
             pltpu.VMEM((2 * NB * BS, BS), bf16),
             pltpu.VMEM((2 * NB * BS, BS), bf16),
-            pltpu.VMEM((row_count, LON, D), bf16),
-            pltpu.VMEM((row_count, LON, FF), bf16),
-            pltpu.VMEM((FF, rank), bf16),
+            pltpu.VMEM(grid_shape, bf16),
+            pltpu.VMEM((FF // 128, LON, row_count, 128), bf16),
+            pltpu.VMEM((rank, FF), bf16),
             pltpu.VMEM((2 * NB * BS, 4 * BS), bf16),
             pltpu.VMEM((2 * NB * BS, 4 * BS), bf16),
             pltpu.VMEM((modes, D), bf16),
@@ -619,34 +646,34 @@
             pltpu.VMEM((space_count, 4 * BS // space_count, 256), bf16),
             pltpu.VMEM((space_count, 4 * BS // space_count, 256), bf16),
             pltpu.VMEM((space_count, 4 * BS // space_count, 256), bf16),
-            pltpu.SemaphoreType.DMA((7,)),
+            pltpu.SemaphoreType.DMA((3 * (D // 128) + FF // 128 + 8,)),
             pltpu.SemaphoreType.DMA((copies,)),
             pltpu.SemaphoreType.DMA((copies,)),
         ],
         compiler_params=pltpu.CompilerParams(
-            collective_id=0, has_side_effects=True, vmem_limit_bytes=48 * 1024 * 1024
+            collective_id=0, has_side_effects=True, vmem_limit_bytes=60 * 1024 * 1024
         ),
         name="fused_filter_sketch",
     )(
-        grad_mid.reshape(row_count, LON, D),
+        grad_mid.transpose(0, 2, 1, 3).reshape(LON, row_count, D),
         spectrum.reshape(modes, D),
         filter_inner.reshape(2 * NB * BS, BS),
         filter_outer.reshape(2 * NB * BS, BS),
         cutoff.reshape(1, KLON),
-        normed_mid.reshape(row_count, LON, D),
-        hidden_grad.reshape(row_count, LON, FF),
-        power_start,
+        normed_mid.transpose(0, 2, 1, 3).reshape(LON, row_count, D),
+        hidden_grad.transpose(0, 2, 1, 3).reshape(LON, row_count, FF),
+        power_start.T,
         lon_table,
         spread,
         lat_table,
         back_table,
     )
-    odd = lax.rem(lax.axis_index("dp"), 2) == 1
-    width = 2 * BS
-    weights = jnp.where(odd, weight_out[:, 256 - width :], weight_out[:, :width])
-    weights = weights.reshape(4, BS, 2, BS).transpose(0, 2, 1, 3)
-    right = jnp.where(odd, right_out[:, 256 - width :], right_out[:, :width])
-    return (grid_out.reshape(grad_mid.shape), weights[:2], weights[2:], left_out.T, right.T)
+    samples = data_count * row_count * space_count
+    weights = weight_out * (1.0 / math.sqrt(samples * KLON))
+    left = (left_out * scale_out).T
+    right = right_out.T * (1.0 / math.sqrt(samples * LON))
+    grid = grid_out.reshape(1, LON, row_count, D).transpose(0, 2, 1, 3)
+    return (grid, weights[:2], weights[2:], left, right)
 
 
 def solution(mesh):

time: 55.3 us -> 49.9 us (0.902)
  local copies, waits for them, and re-layouts: 11.9 us -> 1.58 us
  other arithmetic: 0.86 us -> 4.91 us
  Pallas kernels: 41.6 us -> 42.5 us
    unnamed x30 -> x3, local copies, waits for them, and re-layouts: 9.83 us -> 0.81 us
    mul x0 -> x2, other arithmetic: none -> 2.41 us  [the longest x1 1.38 us: fused_body(): right = right_out.T * (1.0 / math.sqrt(samples * LON))]
    reshape x2 -> x0, local copies, waits for them, and re-layouts: 1.74 us -> none  [the longest x1 1.48 us: fused_body(): normed_mid.reshape(row_count, LON, D)]
    pallas_call x1, Pallas kernels: 41.6 us -> 42.5 us  [fused_body(): pl.pallas_call(fused_kernel, out_shape=(jax.ShapeDtypeStruct((LON, row_co...]
    transpose x1, other arithmetic: 0.69 us -> 1.61 us  [fused_body(): left = (left_out * scale_out).T]
    pallas_call x0 -> x1, other arithmetic: none -> 0.89 us  [fused_body(): pl.pallas_call(fused_kernel, out_shape=(jax.ShapeDtypeStruct((LON, row_co...]
    slice x1, local copies, waits for them, and re-layouts: 0.15 us -> 0.77 us  [fused_body(): return (grid, weights[:2], weights[2:], left, right)]
where the time goes in v2:
time: 49.9 us; the launch traced here: 49.7 us
  Pallas kernels  42.5 us (85%)
  other arithmetic  4.91 us (10%)
  local copies, waits for them, and re-layouts  1.58 us (3%)
  between operations  0.66 us (1%)
    pallas_call x1, Pallas kernels, fused_body(): pl.pallas_call(fused_kernel, out_shape=(jax.ShapeDtypeStruct((LON, row_co...  42.5 us
    transpose x1, other arithmetic, fused_body(): left = (left_out * scale_out).T  1.61 us
    mul x1, other arithmetic, fused_body(): right = right_out.T * (1.0 / math.sqrt(samples * LON))  1.38 us
    mul x1, other arithmetic, fused_body(): weights = weight_out * (1.0 / math.sqrt(samples * KLON))  1.03 us

profile of v2, /device:TPU:0, one launch (start us, length us, event | category | flops | bytes accessed | tf_op | source)
XLA Modules:
  0.0 49.7 jit_solution(10253863056581265876)
XLA Ops:
  0.6 42.5 %fused_filter_sketch.1 = (bf16[180,2,768]{2,1,0:T(2,128)(2,1)}, f32[4,2,96,96]{3,2,1,0:T(8,128)}, f32[32,768]{1,0:T(8,128)}, f32[32,1]{1,0:T(8,128)}, f32[32,192]{1,0:T(8,128)}) custom-call(bf16[180,2,768]{2,1,0:T(2,128)(2,1)} %bitcast.23, bf16[256,768]{1,0:T(8,128)(2,1)} %bitcast.25, bf16[1536,96]{1,0:T(8,128)(2,1)} %bitcast.26, bf16[1536,96]{1,0:T(8,128)(2,1)} %bitcast.27, ...), custom_call_target="tpu_custom_call" | custom-call | tf_op jit(solution)/shard_map/fused_filter_sketch/pallas_call | solution.py:598
  43.2 0.0 copy-start
  43.2 0.9 %reduce = f32[32]{0:T(128)S(1)} reduce(f32[32,1]{1,0:T(8,128)} %get-tuple-element.13, f32[]{:T(128)} %constant.20), dimensions={1}, to_apply=%get-tuple-element.13.reduce_sub_computation | reduce | bytes 260 | tf_op jit(solution)/shard_map/fused_filter_sketch/pallas_call | solution.py:598
  44.1 1.6 %multiply_bitcast_fusion = f32[768,32]{0,1:T(8,128)} fusion(f32[32,768]{1,0:T(8,128)} %get-tuple-element.12, f32[32]{0:T(128)S(1)} %reduce), kind=kLoop, calls=%fused_computation.1 | loop fusion | flops 24576 | bytes 196736 | tf_op jit(solution)/shard_map/transpose | solution.py:673
  45.7 1.0 %broadcast_multiply_fusion = f32[4,2,96,96]{3,2,1,0:T(8,128)S(1)} fusion(f32[4,2,96,96]{3,2,1,0:T(8,128)} %get-tuple-element.11), kind=kLoop, calls=%fused_computation | loop fusion | flops 73728 | bytes 589824 | tf_op jit(solution)/shard_map/mul | solution.py:672
  46.7 0.8 %fusion = (f32[2,2,96,96]{3,2,1,0:T(8,128)}, f32[2,2,96,96]{3,2,1,0:T(8,128)}) fusion(f32[4,2,96,96]{3,2,1,0:T(8,128)S(1)} %broadcast_multiply_fusion), kind=kLoop, calls=%fused_computation.3 | loop fusion | bytes 589824 | tf_op jit(solution)/shard_map/slice | solution.py:676
  47.5 1.4 %multiply_bitcast_fusion.1 = f32[192,32]{0,1:T(8,128)} fusion(f32[32,192]{1,0:T(8,128)} %get-tuple-element.14), kind=kLoop, calls=%fused_computation.2 | loop fusion | flops 6144 | bytes 49152 | tf_op jit(solution)/shard_map/mul | solution.py:674
  48.9 0.0 copy-done
  48.9 0.8 %copy.18 = bf16[1,2,180,768]{3,1,2,0:T(2,128)(2,1)} copy(bf16[1,2,180,768]{3,1,2,0:T(2,128)(2,1)S(1)} %bitcast.22) | data formatting | bytes 1105920
Async XLA Ops:
  43.2 5.7 %copy-start = (bf16[180,2,768]{2,1,0:T(2,128)(2,1)S(1)}, bf16[180,2,768]{2,1,0:T(2,128)(2,1)}, u32[]{:S(2)}) copy-start(bf16[180,2,768]{2,1,0:T(2,128)(2,1)} %get-tuple-element.10) | copy-start | bytes 1658884

commit v3 on v2

--- a/solution.py
+++ b/solution.py
@@ -238,9 +238,9 @@
     lat_hbm,
     back_hbm,
     grid_hbm_out,
-    weight_out,
+    inner_out,
+    outer_out,
     left_out,
-    scale_out,
     right_out,
     lon_ref,
     spread_ref,
@@ -276,7 +276,6 @@
     right_cross,
     wide_send,
     wide_recv,
-    half_send,
     half_recv,
     quarter_send,
     quarter_recv,
@@ -287,7 +286,7 @@
 ):
     bf16, f32 = jnp.bfloat16, jnp.float32
     space, data = lax.axis_index("space"), lax.axis_index("dp")
-    space_count, data_count = mode_send.shape[0], sketch_recv.shape[0]
+    space_count, data_count = mode_send.shape[1], sketch_recv.shape[0]
     core, chip = lax.rem(data, 2), lax.div(data, 2)
     row_count = grid_ref.shape[2]
     token_count = grid_ref.shape[1] * row_count
@@ -383,11 +382,22 @@
         for copy in copies:
             copy.wait_recv()
 
+    group = 4 * BS
+    groups = [slice(index * group, (index + 1) * group) for index in range(NB // 4)]
     finish(grid_loads)
-    mode_send[...] = mxu(lon_ref[...], tokens(grid_ref)).astype(bf16).reshape(mode_send.shape)
-    pl.semaphore_wait(barrier, space_count + data_count - 2)
-    mode_copies = over_space(lambda peer: mode_send.at[peer], mode_recv.at[space])
-    mode_recv[space] = mode_send[space]
+    grid_tokens = tokens(grid_ref)
+    mode_copies = []
+    for index, lanes in enumerate(groups):
+        modes = mxu(lon_ref[...], grid_tokens[:, lanes]).astype(bf16)
+        mode_send[index] = modes.reshape(mode_send.shape[1:])
+        if index == 0:
+            pl.semaphore_wait(barrier, space_count + data_count - 2)
+        mode_copies.append(
+            over_space(
+                lambda peer, index=index: mode_send.at[index, peer], mode_recv.at[index, space]
+            )
+        )
+        mode_recv[index, space] = mode_send[index, space]
 
     finish(hidden_loads)
     probe = mxu(tokens(hidden_ref), start_ref[...], NT).astype(bf16)
@@ -399,7 +409,6 @@
     sketch_copies = over_data(lambda peer: sketch_local.at[peer], sketch_recv.at[data])
     sketch_recv[data] = sketch_local[data]
 
-    group = 4 * BS
     column = lax.broadcasted_iota(jnp.int32, (BS, group), 1)
     place = lax.broadcasted_iota(jnp.int32, (BS, group), 0)
     repeat = jnp.where(lax.rem(column, BS) == place, 1.0, 0.0).astype(bf16)
@@ -414,7 +423,6 @@
         first = (part * (NB // 4) + index) * group
         return ref[first : first + group, :]
 
-    groups = [slice(index * group, (index + 1) * group) for index in range(NB // 4)]
     for index, lanes in enumerate(groups):
         values = spectrum_ref[:, lanes]
         by_real = mxu(values, wide_weight(inner_wide, 0, index))
@@ -455,10 +463,14 @@
     sketch_full[data] = part
     full_copies = over_data(lambda peer: sketch_full.at[data], sketch_full.at[data])
 
-    arrive(mode_copies)
-    arrived = mode_recv[...].reshape(full, D)
-    cot_ref[...] = (mxu(lat_ref[...], arrived) * weight).astype(bf16)
+    lane_block = lax.div(lax.broadcasted_iota(jnp.int32, (BS, group), 1), BS)
+    back_copies = []
+    core_copies = []
+    pair = data + 1 - 2 * core
     for index, lanes in enumerate(groups):
+        arrive(mode_copies[index])
+        arrived = mode_recv[index].reshape(full, group)
+        cot_ref[:, lanes] = (mxu(lat_ref[...], arrived) * weight).astype(bf16)
         values = cot_ref[:, lanes]
         by_real = mxu(values, wide_weight(outer_wide, 0, index), NT)
         by_imag = mxu(values, wide_weight(outer_wide, 1, index), NT)
@@ -471,28 +483,41 @@
         by_imag = mxu(values, wide_weight(inner_wide, 1, index), NT)
         xg_ref[:half, lanes] = (by_real[:half] + by_imag[half:]).astype(bf16)
         xg_ref[half:, lanes] = (by_real[half:] - by_imag[:half]).astype(bf16)
-    back_send[...] = mxu(back_ref[...], xg_ref[...]).astype(bf16).reshape(back_send.shape)
-    back_copies = over_space(lambda peer: back_send.at[peer], back_recv.at[space])
-    back_recv[space] = back_send[space]
-
-    lane_block = lax.div(lax.broadcasted_iota(jnp.int32, (BS, group), 1), BS)
-    for first, left, right in ((0, spectrum_ref, hid_ref), (2, act_ref, cot_ref)):
-        for index, lanes in enumerate(groups):
+        back = mxu(back_ref[...], xg_ref[:, lanes]).astype(bf16)
+        back_send[index] = back.reshape(back_send.shape[1:])
+        back_copies += over_space(
+            lambda peer, index=index: back_send.at[index, peer], back_recv.at[index, space]
+        )
+        back_recv[index, space] = back_send[index, space]
+
+        for first, left, right in ((0, spectrum_ref, hid_ref), (1, act_ref, cot_ref)):
             values = left[:, lanes]
             turned = jnp.concatenate([right[half:, lanes], -right[:half, lanes]], axis=0)
-            for part, other in ((0, right[:, lanes]), (1, turned)):
+            parts = []
+            for other in (right[:, lanes], turned):
                 product = mxu(values, other, TN)
                 compact = jnp.zeros((BS, group), f32)
                 for block in range(4):
                     compact = jnp.where(
                         lane_block == block, product[block * BS : (block + 1) * BS], compact
                     )
-                compact = compact.astype(bf16)
-                rows = slice((first + part) * BS, (first + part + 1) * BS)
-                wide_send[0, index, rows, :] = compact[:, :256]
-                wide_send[1, index, rows, :] = compact[:, 128:]
-    pair = data + 1 - 2 * core
-    core_copy = push(wide_send.at[1 - core], wide_recv, {"dp": pair})
+                parts.append(compact)
+            rows = slice(first * BS, (first + 1) * BS)
+            low = lane_block < 2
+            wide_send[0, index, rows, :] = jnp.where(
+                low, parts[0], pltpu.roll(parts[1], 2 * BS, 1)
+            ).astype(bf16)
+            wide_send[1, index, rows, :] = jnp.where(
+                low, pltpu.roll(parts[0], 2 * BS, 1), parts[1]
+            ).astype(bf16)
+        core_copies.append(
+            push(wide_send.at[1 - core, index], wide_recv.at[index], {"dp": pair})
+        )
+
+    arrive(core_copies)
+    mine = wide_send[core].astype(f32) + wide_recv[...].astype(f32)
+    wide_recv[...] = mine.astype(bf16)
+    chip_copy = push(wide_recv.at[1 - chip], half_recv, {"dp": lax.rem(data + 2, data_count)})
 
     arrive(full_copies)
     sketch = sketch_full[...].reshape(data_count * rank_part, D)
@@ -511,14 +536,15 @@
     )
     diagonal = jnp.sum(jnp.where(eye, gram, 0.0), axis=1, keepdims=True)
     scale = 1.0 / jnp.sqrt(diagonal)
-    left_out[...] = sketch
-    scale_out[...] = scale
-    left_round = (sketch * scale).astype(bf16)
-
-    core_copy.wait_recv()
-    mine = wide_send[core].astype(f32) + wide_recv[...].astype(f32)
-    wide_recv[...] = mine.astype(bf16)
-    chip_copy = push(wide_recv.at[1 - chip], half_recv, {"dp": lax.rem(data + 2, data_count)})
+    left_factor = sketch * scale
+    left_out[...] = left_factor
+    left_round = left_factor.astype(bf16)
+
+    chip_copy.wait_recv()
+    mine = wide_recv[chip].astype(f32) + half_recv[...].astype(f32)
+    quarter_send[...] = mine.astype(bf16).reshape(quarter_send.shape)
+    quarter_copies = over_space(lambda peer: quarter_send.at[peer], quarter_recv.at[space])
+    quarter_recv[space] = quarter_send[space]
 
     mixed = mxu(left_round, tokens(normed_ref), NT).astype(bf16)
     total = mxu(mixed, tokens(hidden_ref)).astype(bf16)
@@ -529,12 +555,6 @@
     right_copies = over_data(lambda peer: right_send.at[peer], right_recv.at[data])
     right_recv[data] = right_send[data]
 
-    chip_copy.wait_recv()
-    mine = wide_recv[chip].astype(f32) + half_recv[...].astype(f32)
-    quarter_send[...] = mine.astype(bf16).reshape(quarter_send.shape)
-    quarter_copies = over_space(lambda peer: quarter_send.at[peer], quarter_recv.at[space])
-    quarter_recv[space] = quarter_send[space]
-
     arrive(right_copies)
     part = right_recv[0].astype(f32)
     for peer in range(1, data_count):
@@ -543,17 +563,6 @@
     last_copies = over_space(lambda peer: right_part.at[peer], right_cross.at[space])
     right_cross[space] = right_part[space]
 
-    arrive(back_copies)
-    arrived = back_recv[...].reshape(full, D)
-    grid_view = grid_out.reshape(grid_out.shape[0], token_count, 128)
-    result = (tokens(grid_ref).astype(f32) + mxu(spread_ref[...], arrived)).astype(bf16)
-    for index in range(grid_out.shape[0]):
-        grid_view[index] = result[:, index * 128 : (index + 1) * 128]
-    stores = [
-        load(grid_out.at[index], grid_hbm_out.at[:, :, index * 128 : (index + 1) * 128])
-        for index in range(grid_out.shape[0])
-    ]
-
     arrive(quarter_copies)
     part = quarter_recv[0].astype(f32)
     for peer in range(1, space_count):
@@ -561,19 +570,38 @@
     piece_all[space] = part.astype(bf16)
     piece_copies = over_space(lambda peer: piece_all.at[space], piece_all.at[space])
 
+    arrive(back_copies)
+    grid_view = grid_out.reshape(grid_out.shape[0], token_count, 128)
+    stores = []
+    grid_tokens_again = tokens(grid_ref)
+    for index, lanes in enumerate(groups):
+        arrived = back_recv[index].reshape(full, group)
+        result = grid_tokens_again[:, lanes].astype(f32) + mxu(spread_ref[...], arrived)
+        result = result.astype(bf16)
+        for tile in range(group // 128):
+            place = index * (group // 128) + tile
+            grid_view[place] = result[:, tile * 128 : (tile + 1) * 128]
+            stores.append(
+                load(
+                    grid_out.at[place],
+                    grid_hbm_out.at[:, :, place * 128 : (place + 1) * 128],
+                )
+            )
+
     arrive(last_copies)
     part = right_cross[0].astype(f32)
     for peer in range(1, space_count):
         part = part + right_cross[peer].astype(f32)
     part = jnp.where(core == 1, pltpu.roll(part, 192, 1), part)
-    right_out[...] = part[:, : 2 * BS]
+    right_out[...] = part[:, : 2 * BS] * (1.0 / math.sqrt(data_count * lat_count * LON))
 
     arrive(piece_copies)
-    for index in range(space_count):
-        part = piece_all[index].astype(f32)
-        part = jnp.where(core == 1, pltpu.roll(part, 192, 1), part)
-        weight_out[index, 0] = part[:, :BS]
-        weight_out[index, 1] = pltpu.roll(part, 256 - BS, 1)[:, :BS]
+    result = piece_all[...].reshape(2 * BS, group).astype(f32)
+    result = result * (1.0 / math.sqrt(data_count * lat_count * KLON))
+    for place in range(4):
+        turned = result if place == 0 else pltpu.roll(result, group - place * BS, 1)
+        inner_out[place // 2, place % 2] = turned[:BS, :BS]
+        outer_out[place // 2, place % 2] = turned[BS:, :BS]
     finish(stores)
     for copy in pending:
         copy.wait_send()
@@ -592,16 +620,16 @@
     lon_table, spread, lat_table, back_table = fused_tables(space_count, row_count)
     vmem = pl.BlockSpec(memory_space=pltpu.VMEM)
     anywhere = pl.BlockSpec(memory_space=pl.ANY)
-    slab = (space_count, row_count * 2 * mode_local, D)
-    copies = 5 * (space_count - 1) + 3 * (data_count - 1) + 2 + (space_count - 1)
+    slab = (NB // 4, space_count, row_count * 2 * mode_local, 4 * BS)
+    copies = 8 * (space_count - 1) + 3 * (data_count - 1) + 3
     grid_shape = (D // 128, LON, row_count, 128)
-    grid_out, weight_out, left_out, scale_out, right_out = pl.pallas_call(
+    grid_out, inner_out, outer_out, left_out, right_out = pl.pallas_call(
         fused_kernel,
         out_shape=(
             jax.ShapeDtypeStruct((LON, row_count, D), bf16),
-            jax.ShapeDtypeStruct((4, 2, BS, BS), f32),
+            jax.ShapeDtypeStruct((2, 2, BS, BS), f32),
+            jax.ShapeDtypeStruct((2, 2, BS, BS), f32),
             jax.ShapeDtypeStruct((rank, D), f32),
-            jax.ShapeDtypeStruct((rank, 1), f32),
             jax.ShapeDtypeStruct((rank, 2 * BS), f32),
         ),
         in_specs=[anywhere] * 4 + [vmem] + [anywhere] * 7,
@@ -639,13 +667,12 @@
             pltpu.VMEM((data_count, space_count, rank, 256), bf16),
             pltpu.VMEM((space_count, rank, 256), bf16),
             pltpu.VMEM((space_count, rank, 256), bf16),
-            pltpu.VMEM((2, 2, 4 * BS, 256), bf16),
-            pltpu.VMEM((2, 4 * BS, 256), bf16),
-            pltpu.VMEM((4 * BS, 256), bf16),
-            pltpu.VMEM((4 * BS, 256), bf16),
-            pltpu.VMEM((space_count, 4 * BS // space_count, 256), bf16),
-            pltpu.VMEM((space_count, 4 * BS // space_count, 256), bf16),
-            pltpu.VMEM((space_count, 4 * BS // space_count, 256), bf16),
+            pltpu.VMEM((2, 2, 2 * BS, 4 * BS), bf16),
+            pltpu.VMEM((2, 2 * BS, 4 * BS), bf16),
+            pltpu.VMEM((2 * BS, 4 * BS), bf16),
+            pltpu.VMEM((space_count, 2 * BS // space_count, 4 * BS), bf16),
+            pltpu.VMEM((space_count, 2 * BS // space_count, 4 * BS), bf16),
+            pltpu.VMEM((space_count, 2 * BS // space_count, 4 * BS), bf16),
             pltpu.SemaphoreType.DMA((3 * (D // 128) + FF // 128 + 8,)),
             pltpu.SemaphoreType.DMA((copies,)),
             pltpu.SemaphoreType.DMA((copies,)),
@@ -668,12 +695,8 @@
         lat_table,
         back_table,
     )
-    samples = data_count * row_count * space_count
-    weights = weight_out * (1.0 / math.sqrt(samples * KLON))
-    left = (left_out * scale_out).T
-    right = right_out.T * (1.0 / math.sqrt(samples * LON))
     grid = grid_out.reshape(1, LON, row_count, D).transpose(0, 2, 1, 3)
-    return (grid, weights[:2], weights[2:], left, right)
+    return (grid, inner_out, outer_out, left_out.T, right_out.T)
 
 
 def solution(mesh):

time: 49.9 us -> 49.6 us (level)
  local copies, waits for them, and re-layouts: 1.58 us -> 8.38 us
  other arithmetic: 4.91 us -> 0 us
  Pallas kernels: 42.5 us -> 40.1 us
    unnamed x3 -> x5, local copies, waits for them, and re-layouts: 0.81 us -> 8.38 us
    pallas_call x1, Pallas kernels: 42.5 us -> 40.1 us  [fused_body(): pl.pallas_call(fused_kernel, out_shape=(jax.ShapeDtypeStruct((LON, row_co...]
    mul x2 -> x0, other arithmetic: 2.41 us -> none  [the longest x1 1.38 us: fused_body(): right = right_out.T * (1.0 / math.sqrt(samples * LON))]
    transpose x1 -> x0, other arithmetic: 1.61 us -> none  [fused_body(): left = (left_out * scale_out).T]
    pallas_call x1 -> x0, other arithmetic: 0.89 us -> none  [fused_body(): pl.pallas_call(fused_kernel, out_shape=(jax.ShapeDtypeStruct((LON, row_co...]
    slice x1 -> x0, local copies, waits for them, and re-layouts: 0.77 us -> none  [fused_body(): return (grid, weights[:2], weights[2:], left, right)]
where the time goes in v3:
time: 49.6 us; the launch traced here: 49.1 us
  Pallas kernels  40.1 us (81%)
  local copies, waits for them, and re-layouts  8.38 us (17%)
  between operations  0.64 us (1%)
    pallas_call x1, Pallas kernels, fused_body(): pl.pallas_call(fused_kernel, out_shape=(jax.ShapeDtypeStruct((LON, row_co...  40.1 us
    unnamed x5, local copies, waits for them, and re-layouts  8.38 us

profile of v3, /device:TPU:0, one launch (start us, length us, event | category | flops | bytes accessed | tf_op | source)
XLA Modules:
  0.0 49.1 jit_solution(2600785915045789270)
XLA Ops:
  0.6 40.1 %fused_filter_sketch.1 = (bf16[180,2,768]{2,1,0:T(2,128)(2,1)}, f32[2,2,96,96]{3,2,1,0:T(8,128)}, f32[2,2,96,96]{3,2,1,0:T(8,128)}, f32[32,768]{1,0:T(8,128)}, f32[32,192]{1,0:T(8,128)}) custom-call(bf16[180,2,768]{2,1,0:T(2,128)(2,1)} %bitcast.21, bf16[256,768]{1,0:T(8,128)(2,1)} %bitcast.23, bf16[1536,96]{1,0:T(8,128)(2,1)} %bitcast.24, ...), custom_call_target="tpu_custom_call" | custom-call | tf_op jit(solution)/shard_map/fused_filter_sketch/pallas_call | solution.py:626
  40.7 2.2 %copy.22 = bf16[1,2,180,768]{3,1,2,0:T(2,128)(2,1)} copy(bf16[1,2,180,768]{3,1,2,0:T(2,128)(2,1)} %bitcast.20) | data formatting | bytes 1105920
  43.0 1.6 %copy.23 = f32[2,2,96,96]{3,2,1,0:T(8,128)} copy(f32[2,2,96,96]{3,2,1,0:T(8,128)} %get-tuple-element.21) | data formatting | bytes 294912
  44.6 1.6 %copy.24 = f32[2,2,96,96]{3,2,1,0:T(8,128)} copy(f32[2,2,96,96]{3,2,1,0:T(8,128)} %get-tuple-element.22) | data formatting | bytes 294912
  46.2 1.5 %copy.25 = f32[768,32]{0,1:T(8,128)} copy(f32[768,32]{0,1:T(8,128)} %bitcast.27) | data formatting | bytes 196608
  47.8 1.4 %copy.26 = f32[192,32]{0,1:T(8,128)} copy(f32[192,32]{0,1:T(8,128)} %bitcast.28) | data formatting | bytes 49152

commit v4 on v3

--- a/solution.py
+++ b/solution.py
@@ -620,6 +620,7 @@
     lon_table, spread, lat_table, back_table = fused_tables(space_count, row_count)
     vmem = pl.BlockSpec(memory_space=pltpu.VMEM)
     anywhere = pl.BlockSpec(memory_space=pl.ANY)
+    held = pl.BlockSpec(memory_space=pltpu.HBM)
     slab = (NB // 4, space_count, row_count * 2 * mode_local, 4 * BS)
     copies = 8 * (space_count - 1) + 3 * (data_count - 1) + 3
     grid_shape = (D // 128, LON, row_count, 128)
@@ -632,7 +633,7 @@
             jax.ShapeDtypeStruct((rank, D), f32),
             jax.ShapeDtypeStruct((rank, 2 * BS), f32),
         ),
-        in_specs=[anywhere] * 4 + [vmem] + [anywhere] * 7,
+        in_specs=[held] * 4 + [vmem] + [held] * 7,
         out_specs=(anywhere,) + (vmem,) * 4,
         scratch_shapes=[
             pltpu.VMEM((modes, LON * row_count), bf16),
@@ -678,7 +679,7 @@
             pltpu.SemaphoreType.DMA((copies,)),
         ],
         compiler_params=pltpu.CompilerParams(
-            collective_id=0, has_side_effects=True, vmem_limit_bytes=60 * 1024 * 1024
+            collective_id=0, has_side_effects=True, vmem_limit_bytes=40 * 1024 * 1024
         ),
         name="fused_filter_sketch",
     )(

time: 49.6 us -> 59.3 us (1.20)
  local copies, waits for them, and re-layouts: 8.38 us -> 15.4 us
  Pallas kernels: 40.1 us -> 42.7 us
    unnamed x5 -> x29, local copies, waits for them, and re-layouts: 8.38 us -> 15.4 us
    pallas_call x1, Pallas kernels: 40.1 us -> 42.7 us  [fused_body(): pl.pallas_call(fused_kernel, out_shape=(jax.ShapeDtypeStruct((LON, row_co...]
where the time goes in v4:
time: 59.3 us; the launch traced here: 58.7 us
  Pallas kernels  42.7 us (72%)
  local copies, waits for them, and re-layouts  15.4 us (26%)
  between operations  0.66 us (1%)
    pallas_call x1, Pallas kernels, fused_body(): pl.pallas_call(fused_kernel, out_shape=(jax.ShapeDtypeStruct((LON, row_co...  42.7 us
    unnamed x29, local copies, waits for them, and re-layouts  15.4 us

profile of v4, /device:TPU:0, one launch (start us, length us, event | category | flops | bytes accessed | tf_op | source)
XLA Modules:
  0.0 58.7 jit_solution(4640869695914027317)
XLA Ops:
  0.6 0.0 copy-start
  0.6 1.6 %copy-done = bf16[1,2,180,3072]{3,1,2,0:T(2,128)(2,1)S(1)} copy-done((bf16[1,2,180,3072]{3,1,2,0:T(2,128)(2,1)S(1)}, bf16[1,2,180,3072]{3,1,2,0:T(2,128)(2,1)}, u32[]{:S(2)}) %copy-start) | copy-done | bytes 2211864
  2.3 0.0 copy-start.1
  2.3 1.0 %copy-done.1 = bf16[1,2,180,768]{3,1,2,0:T(2,128)(2,1)S(1)} copy-done((bf16[1,2,180,768]{3,1,2,0:T(2,128)(2,1)S(1)}, bf16[1,2,180,768]{3,1,2,0:T(2,128)(2,1)}, u32[]{:S(2)}) %copy-start.1) | copy-done | bytes 552984
  3.3 1.0 %copy-done.2 = bf16[1,2,180,768]{3,1,2,0:T(2,128)(2,1)S(1)} copy-done((bf16[1,2,180,768]{3,1,2,0:T(2,128)(2,1)S(1)}, bf16[1,2,180,768]{3,1,2,0:T(2,128)(2,1)}, u32[]{:S(2)}) %copy-start.2) | copy-done | bytes 552984
  4.4 0.0 copy-start.3
  4.4 1.0 %copy-done.3 = bf16[2,1,8,16,768]{4,3,2,1,0:T(8,128)(2,1)S(1)} copy-done((bf16[2,1,8,16,768]{4,3,2,1,0:T(8,128)(2,1)S(1)}, bf16[2,1,8,16,768]{4,3,2,1,0:T(8,128)(2,1)}, u32[]{:S(2)}) %copy-start.3) | copy-done | bytes 393240
  5.4 0.0 copy-start.4
  5.4 1.0 %copy-done.4 = bf16[2,8,96,96]{3,2,1,0:T(8,128)(2,1)S(1)} copy-done((bf16[2,8,96,96]{3,2,1,0:T(8,128)(2,1)S(1)}, bf16[2,8,96,96]{3,2,1,0:T(8,128)(2,1)}, u32[]{:S(2)}) %copy-start.4) | copy-done | bytes 294936
  6.4 0.0 copy-start.5
  6.4 1.0 %copy-done.5 = bf16[2,8,96,96]{3,2,1,0:T(8,128)(2,1)S(1)} copy-done((bf16[2,8,96,96]{3,2,1,0:T(8,128)(2,1)S(1)}, bf16[2,8,96,96]{3,2,1,0:T(8,128)(2,1)}, u32[]{:S(2)}) %copy-start.5) | copy-done | bytes 294936
  7.4 0.0 copy-start.6
  7.4 0.9 %copy-done.6 = bf16[3072,32]{0,1:T(8,128)(2,1)S(1)} copy-done((bf16[3072,32]{0,1:T(8,128)(2,1)S(1)}, bf16[3072,32]{0,1:T(8,128)(2,1)}, u32[]{:S(2)}) %copy-start.6) | copy-done | bytes 196632
  8.3 0.9 %copy-done.7 = bf16[256,360]{1,0:T(8,128)(2,1)S(1)} copy-done((bf16[256,360]{1,0:T(8,128)(2,1)S(1)}, bf16[256,360]{1,0:T(8,128)(2,1)}, u32[]{:S(2)}) %copy-start.7) | copy-done | bytes 184344
  9.2 0.9 %copy-done.8 = bf16[360,256]{1,0:T(8,128)(2,1)S(1)} copy-done((bf16[360,256]{1,0:T(8,128)(2,1)S(1)}, bf16[360,256]{1,0:T(8,128)(2,1)}, u32[]{:S(2)}) %copy-start.8) | copy-done | bytes 184344
  10.1 0.9 %copy-done.9 = bf16[256,256]{1,0:T(8,128)(2,1)S(1)} copy-done((bf16[256,256]{1,0:T(8,128)(2,1)S(1)}, bf16[256,256]{1,0:T(8,128)(2,1)}, u32[]{:S(2)}) %copy-start.9) | copy-done | bytes 131096
  11.0 0.9 %copy-done.10 = bf16[256,256]{1,0:T(8,128)(2,1)S(1)} copy-done((bf16[256,256]{1,0:T(8,128)(2,1)S(1)}, bf16[256,256]{1,0:T(8,128)(2,1)}, u32[]{:S(2)}) %copy-start.10) | copy-done | bytes 131096
  11.9 0.7 %copy-done.11 = s32[64]{0:T(128)S(1)} copy-done((s32[64]{0:T(128)S(1)}, s32[64]{0:T(128)}, u32[]{:S(2)}) %copy-start.11) | copy-done | bytes 280
  12.6 42.7 %fused_filter_sketch.1 = (bf16[180,2,768]{2,1,0:T(2,128)(2,1)S(1)}, f32[2,2,96,96]{3,2,1,0:T(8,128)S(1)}, f32[2,2,96,96]{3,2,1,0:T(8,128)S(1)}, f32[32,768]{1,0:T(8,128)S(1)}, f32[32,192]{1,0:T(8,128)S(1)}) custom-call(bf16[180,2,768]{2,1,0:T(2,128)(2,1)S(1)} %bitcast.21, bf16[256,768]{1,0:T(8,128)(2,1)S(1)} %bitcast.23, bf16[1536,96]{1,0:T(8,128)(2,1)S(1)} %bitcast.24, ...), custom_call_target="tpu_custom_call" | custom-call | tf_op jit(solution)/shard_map/fused_filter_sketch/pallas_call | solution.py:627
  55.3 0.8 %copy.22 = bf16[1,2,180,768]{3,1,2,0:T(2,128)(2,1)} copy(bf16[1,2,180,768]{3,1,2,0:T(2,128)(2,1)S(1)} %bitcast.20) | data formatting | bytes 1105920
  56.1 0.7 %copy.23 = f32[2,2,96,96]{3,2,1,0:T(8,128)} copy(f32[2,2,96,96]{3,2,1,0:T(8,128)S(1)} %get-tuple-element.21) | data formatting | bytes 294912
  56.8 0.7 %copy.24 = f32[2,2,96,96]{3,2,1,0:T(8,128)} copy(f32[2,2,96,96]{3,2,1,0:T(8,128)S(1)} %get-tuple-element.22) | data formatting | bytes 294912
  57.5 0.6 %copy.25 = f32[768,32]{0,1:T(8,128)} copy(f32[768,32]{0,1:T(8,128)S(1)} %bitcast.27) | data formatting | bytes 196608
  58.1 0.6 %copy.26 = f32[192,32]{0,1:T(8,128)} copy(f32[192,32]{0,1:T(8,128)S(1)} %bitcast.28) | data formatting | bytes 49152
  (6 shorter events, 0.0 us)
Async XLA Ops:
  0.6 1.6 %copy-start = (bf16[1,2,180,3072]{3,1,2,0:T(2,128)(2,1)S(1)}, bf16[1,2,180,3072]{3,1,2,0:T(2,128)(2,1)}, u32[]{:S(2)}) copy-start(bf16[1,2,180,3072]{3,1,2,0:T(2,128)(2,1)} %param.18) | copy-start | bytes 6635524
  2.3 1.1 %copy-start.1 = (bf16[1,2,180,768]{3,1,2,0:T(2,128)(2,1)S(1)}, bf16[1,2,180,768]{3,1,2,0:T(2,128)(2,1)}, u32[]{:S(2)}) copy-start(bf16[1,2,180,768]{3,1,2,0:T(2,128)(2,1)} %param.12) | copy-start | bytes 1658884
  3.3 1.1 %copy-start.2 = (bf16[1,2,180,768]{3,1,2,0:T(2,128)(2,1)S(1)}, bf16[1,2,180,768]{3,1,2,0:T(2,128)(2,1)}, u32[]{:S(2)}) copy-start(bf16[1,2,180,768]{3,1,2,0:T(2,128)(2,1)} %param.17) | copy-start | bytes 1658884
  4.4 1.0 %copy-start.3 = (bf16[2,1,8,16,768]{4,3,2,1,0:T(8,128)(2,1)S(1)}, bf16[2,1,8,16,768]{4,3,2,1,0:T(8,128)(2,1)}, u32[]{:S(2)}) copy-start(bf16[2,1,8,16,768]{4,3,2,1,0:T(8,128)(2,1)} %param.13) | copy-start | bytes 1179652
  5.4 1.0 %copy-start.4 = (bf16[2,8,96,96]{3,2,1,0:T(8,128)(2,1)S(1)}, bf16[2,8,96,96]{3,2,1,0:T(8,128)(2,1)}, u32[]{:S(2)}) copy-start(bf16[2,8,96,96]{3,2,1,0:T(8,128)(2,1)} %param.14) | copy-start | bytes 884740
  6.4 1.0 %copy-start.5 = (bf16[2,8,96,96]{3,2,1,0:T(8,128)(2,1)S(1)}, bf16[2,8,96,96]{3,2,1,0:T(8,128)(2,1)}, u32[]{:S(2)}) copy-start(bf16[2,8,96,96]{3,2,1,0:T(8,128)(2,1)} %param.15) | copy-start | bytes 884740
  7.4 0.9 %copy-start.6 = (bf16[3072,32]{0,1:T(8,128)(2,1)S(1)}, bf16[3072,32]{0,1:T(8,128)(2,1)}, u32[]{:S(2)}) copy-start(bf16[3072,32]{0,1:T(8,128)(2,1)} %param.19) | copy-start | bytes 589828
  8.3 0.9 %copy-start.7 = (bf16[256,360]{1,0:T(8,128)(2,1)S(1)}, bf16[256,360]{1,0:T(8,128)(2,1)}, u32[]{:S(2)}) copy-start(bf16[256,360]{1,0:T(8,128)(2,1)} %constant.8.clone.lon_hbm) | copy-start | bytes 552964
  9.2 0.9 %copy-start.8 = (bf16[360,256]{1,0:T(8,128)(2,1)S(1)}, bf16[360,256]{1,0:T(8,128)(2,1)}, u32[]{:S(2)}) copy-start(bf16[360,256]{1,0:T(8,128)(2,1)} %constant.9.clone.spread_hbm) | copy-start | bytes 552964
  10.1 0.9 %copy-start.9 = (bf16[256,256]{1,0:T(8,128)(2,1)S(1)}, bf16[256,256]{1,0:T(8,128)(2,1)}, u32[]{:S(2)}) copy-start(bf16[256,256]{1,0:T(8,128)(2,1)} %constant.11.clone.back_hbm) | copy-start | bytes 393220
  11.0 0.9 %copy-start.10 = (bf16[256,256]{1,0:T(8,128)(2,1)S(1)}, bf16[256,256]{1,0:T(8,128)(2,1)}, u32[]{:S(2)}) copy-start(bf16[256,256]{1,0:T(8,128)(2,1)} %constant.10.clone.lat_hbm) | copy-start | bytes 393220
  11.9 0.7 %copy-start.11 = (s32[64]{0:T(128)S(1)}, s32[64]{0:T(128)}, u32[]{:S(2)}) copy-start(s32[64]{0:T(128)} %param.16) | copy-start | bytes 772
